TPU v7x, 512 devices: a whole 4x8x8 slice. The times are simulated.
512 devices in a mesh: half: 2 (over core), grp: 8 (over y), dev: 32 (over z, x).
Axes of the slice: x: 4, y: 8, z: 8, core: 2. Of those that a mesh axis runs over, the one named last changes fastest.
Arguments:
- panel_block: float32 [16384, 512], P(('half', 'grp', 'dev')), may hold values from -1 to 1, as said below
- trailing: float32 [16384, 4096], P(('half', 'grp'), 'dev'), may hold values from -6 to 6
Outputs:
- triangle: float32 [512, 512], replicated
- projected: float32 [512, 4096], P(None, 'dev')
- remainder: float32 [16384, 4096], P(('half', 'grp'), 'dev')
Inputs may be any that keep to these rules, and one draw needn't show every extreme that they name: `panel_block`: of full column rank.
All inputs are finite; a program needn't handle non-finite values.
Results may differ from a plain program's by a relative error of at most 0.0003.
Values sent between devices are 32-bit elements; how exact they have to be, the bound alone decides.
No kernel may reach another device: no remote copies, remote signals or barrier semaphores. Data moves between devices by JAX's collectives and lax.ppermute only.
A program may use at most 64 MiB of HBM per device.

v0:
```python
import jax
import jax.numpy as jnp
from jax import lax
from jax.experimental import pallas as pl
from jax.experimental.pallas import tpu as pltpu
from jax.sharding import PartitionSpec as P

N = 512
B = 128
V = 8
NB = N // B
NP = B // V
HI = lax.Precision.HIGHEST
F32 = jnp.float32


def across_lanes(v, c):
    return jnp.broadcast_to(v[:, c : c + 1], (V, B))


def across_rows(v, j):
    return jnp.broadcast_to(v[j : j + 1, :], (V, B))


def factor_block(m):
    row = lax.broadcasted_iota(jnp.int32, (V, B), 0)
    lane = lax.broadcasted_iota(jnp.int32, (V, B), 1)
    ups, invs = [], []
    for p in range(NP):
        r0 = p * V
        mp = m[p]
        diag = (lane >= r0) & (lane < r0 + V)
        eye = (lane == row + r0).astype(F32)
        b = [across_lanes(mp, r0 + j) for j in range(V)]
        low, low_e, full = mp, eye, jnp.where(diag, eye, mp)
        dv = jnp.ones((V, B), F32)
        for j in range(V):
            d = across_rows(b[j], j)
            dv = jnp.where(row == j, d, dv)
            mult = b[j] * (1.0 / d)
            mfull = jnp.where(row == j, 0.0, mult)
            mlow = jnp.where(row > j, mult, 0.0)
            for k in range(j + 1, V):
                b[k] = b[k] - mfull * across_rows(b[k], j)
            low = low - mlow * across_rows(low, j)
            low_e = low_e - mlow * across_rows(low_e, j)
            full = full - mfull * across_rows(full, j)
        rs = lax.rsqrt(dv)
        full = full * (1.0 / dv)
        ups.append(jnp.where(lane >= row + r0, low * rs, 0.0))
        invs.append(jnp.where(lane <= row + r0, jnp.where(diag, low_e, low) * rs, 0.0))
        if p + 1 < NP:
            f = [across_rows(full, j) for j in range(V)]
            for q in range(p + 1, NP):
                old = m[q]
                t = [across_lanes(old, r0 + j) * f[j] for j in range(V)]
                s = ((t[0] + t[1]) + (t[2] + t[3])) + ((t[4] + t[5]) + (t[6] + t[7]))
                m[q] = jnp.where(diag, 0.0, old) - s
    return jnp.concatenate(ups, 0), jnp.concatenate(invs, 0)


def mm(a, b, dims=((1,), (0,))):
    return lax.dot_general(a, b, (dims, ((), ())), precision=HI, preferred_element_type=F32)


def factor_kernel(g_ref, r_ref, w_ref, m_ref):
    m_ref[...] = g_ref[...]
    r_ref[...] = jnp.zeros_like(r_ref)
    for k in range(NB):
        o = k * B
        e = o + B
        u, v = factor_block([m_ref[o + V * i : o + V * (i + 1), o:e] for i in range(NP)])
        r_ref[o:e, o:e] = u
        w_ref[o:e, o:e] = v
        if k:
            w_ref[o:e, :o] = mm(v, m_ref[o:e, :o])
        if k + 1 < NB:
            w_ref[o:e, e:] = jnp.zeros((B, N - e), F32)
            ps = mm(v, m_ref[o:e, e:])
            r_ref[o:e, e:] = ps
            lt = mm(m_ref[e:, o:e], v, ((1,), (1,)))
            m_ref[e:, e:] = m_ref[e:, e:] - mm(lt, ps)
            if k:
                m_ref[e:, :o] = m_ref[e:, :o] - mm(lt, w_ref[o:e, :o])
            m_ref[e:, o:e] = -mm(lt, v)


def factor(gram):
    out = jax.ShapeDtypeStruct((N, N), F32)
    vmem = pl.BlockSpec(memory_space=pltpu.VMEM)
    return pl.pallas_call(
        factor_kernel,
        out_shape=(out, out),
        scratch_shapes=[pltpu.VMEM((N, N), F32)],
        in_specs=[vmem],
        out_specs=(vmem, vmem),
        compiler_params=pltpu.CompilerParams(vmem_limit_bytes=32 * 2**20),
        name="factor",
    )(gram)


def sent_to_all(x, axis):
    size = lax.axis_size(axis)
    return lax.all_to_all(jnp.broadcast_to(x[None], (size, *x.shape)), axis, 0, 0, tiled=True)


def summed(x, axis):
    size = lax.axis_size(axis)
    rows = x.shape[0] // size
    share = lax.all_to_all(x.reshape(size, rows, x.shape[1]), axis, 0, 0, tiled=True).sum(0)
    return sent_to_all(share, axis).reshape(x.shape)


def on_device(panel_block, trailing):
    panel_group = sent_to_all(panel_block, "dev").reshape(-1, N)
    gram_part = jnp.dot(panel_group.T, panel_group, precision=HI)
    cross_part = jnp.dot(panel_group.T, trailing, precision=HI)
    total = summed(jnp.concatenate([gram_part, cross_part], 1), ("half", "grp"))
    triangle, inverse = factor(total[:, :N])
    projected = jnp.dot(inverse, total[:, N:], precision=HI)
    solved = jnp.dot(inverse.T, projected, precision=HI)
    remainder = trailing - jnp.dot(panel_group, solved, precision=HI)
    return (triangle, projected, remainder)


def solution(mesh):
    placed = (P(("half", "grp", "dev"), None), P(("half", "grp"), "dev"))
    return jax.shard_map(
        on_device,
        mesh=mesh,
        in_specs=placed,
        out_specs=(P(), P(None, "dev"), P(("half", "grp"), "dev")),
        check_vma=False,
    )
```

profile of v0, /device:TPU:1, one launch (start us, length us, event | category | flops | bytes accessed | tf_op | source)
XLA Modules:
  0.0 180.0 jit_solution(16536210698953453529)
XLA Ops:
  0.6 1.1 broadcast_in_dim.4
  1.7 0.0 copy-start
  1.7 62.3 %all_to_all.15 = f32[32,32,512]{2,1,0:T(8,128)S(1)} all-to-all(f32[32,32,512]{2,1,0:T(8,128)S(1)} %broadcast_in_dim.4), channel_id=1, replica_groups=mesh['half'=2,'grp'=8,'dev'=32] {'dev'}, dimensions={0} | all-to-all | bytes 4194304 | tf_op jit(solution)/shard_map/all_to_all | solution.py:104
  64.1 0.0 copy-done
  64.1 1.4 fusion.3
  65.5 3.5 %convolution_bitcast_fusion = f32[512,512]{0,1:T(8,128)S(1)} fusion(f32[32,32,512]{2,1,0:T(8,128)S(1)} %all_to_all.15), kind=kOutput, calls=%fused_computation | convolution fusion | flops 3221225472 | bytes 3145728 | tf_op jit(solution)/shard_map/dot_general | solution.py:116
  69.0 0.1 pad_maximum_fusion
  69.1 1.5 copy.7
  70.6 41.9 %all_to_all.16 = f32[16,32,640]{2,1,0:T(8,128)S(1)} all-to-all(f32[16,32,640]{2,1,0:T(8,128)} %bitcast.22), channel_id=1, replica_groups=mesh['half'=2,'grp'=8,'dev'=32] {'half','grp'}, dimensions={0} | all-to-all | bytes 2621440 | tf_op jit(solution)/shard_map/all_to_all | solution.py:110
  112.5 0.1 reduce_sum.9
  112.6 1.2 broadcast_in_dim.5
  113.8 5.1 %all-to-all-start.2 = ((f32[16,32,640]{2,1,0:T(8,128)}), f32[16,32,640]{2,1,0:T(8,128)S(1)}, u32[]{:S(2)}, u32[]{:S(2)}) async-start(f32[16,32,640]{2,1,0:T(8,128)} %broadcast_in_dim.5), calls=%async_computation.2 | async-start | bytes 2621440 | tf_op jit(solution)/shard_map/all_to_all | solution.py:104
  118.9 2.0 %copy.8 = f32[1024,128]{0,1:T(8,128)} copy(f32[1024,128]{1,0:T(8,128)} %param.3) | data formatting | bytes 1048576 | tf_op args[1]
  120.9 29.9 %all-to-all-done.2 = f32[16,32,640]{2,1,0:T(8,128)S(1)} async-done(((f32[16,32,640]{2,1,0:T(8,128)}), f32[16,32,640]{2,1,0:T(8,128)S(1)}, u32[]{:S(2)}, u32[]{:S(2)}) %all-to-all-start.2) | async-done | bytes 1310752 | tf_op jit(solution)/shard_map/all_to_all | solution.py:104
  150.8 0.1 slice.8.g_ref
  150.9 0.0 copy-start.1
  150.9 22.9 %factor.1 = (f32[512,512]{1,0:T(8,128)}, f32[512,512]{1,0:T(8,128)S(1)}) custom-call(f32[512,512]{1,0:T(8,128)S(1)} %slice.8.g_ref), custom_call_target="tpu_custom_call" | custom-call | tf_op jit(solution)/shard_map/factor/pallas_call | solution.py:91
  173.9 1.0 fusion.1
  174.9 0.0 copy-start.2
  174.9 1.8 %fusion.4 = f32[512,128]{1,0:T(8,128)S(1)} fusion(f32[512,512]{1,0:T(8,128)S(1)} %get-tuple-element.6, f32[512,128]{1,0:T(8,128)S(1)} %fusion.1), kind=kOutput, calls=%fused_computation.7 | convolution fusion | flops 402653184 | bytes 1572864 | tf_op jit(solution)/shard_map/dot_general | solution.py:121
  176.7 0.0 copy-done.2
  176.7 0.0 copy-done.1
  176.7 2.3 %fusion = f32[1024,128]{0,1:T(8,128)S(1)} fusion(f32[1024,128]{0,1:T(8,128)S(1)} %copy-done.1, f32[512,128]{1,0:T(8,128)S(1)} %fusion.4, f32[1024,512]{1,0:T(8,128)S(1)} %bitcast.19), kind=kOutput, calls=%fused_computation.3 | convolution fusion | flops 805437440 | bytes 3407872 | tf_op jit(solution)/shard_map/dot_general | solution.py:122
  179.0 1.0 copy.9
Async XLA Ops:
  1.7 62.3 %copy-start = (f32[1024,128]{1,0:T(8,128)S(1)}, f32[1024,128]{1,0:T(8,128)}, u32[]{:S(2)}) copy-start(f32[1024,128]{1,0:T(8,128)} %param.3) | copy-start | bytes 1572868
  113.8 37.0 %all-to-all-start.2 = ((f32[16,32,640]{2,1,0:T(8,128)}), f32[16,32,640]{2,1,0:T(8,128)S(1)}, u32[]{:S(2)}, u32[]{:S(2)}) async-start(f32[16,32,640]{2,1,0:T(8,128)} %broadcast_in_dim.5), calls=%async_computation.2 | async-start | bytes 2621440 | tf_op jit(solution)/shard_map/all_to_all | solution.py:104
  150.9 25.8 %copy-start.1 = (f32[1024,128]{0,1:T(8,128)S(1)}, f32[1024,128]{0,1:T(8,128)}, u32[]{:S(2)}) copy-start(f32[1024,128]{0,1:T(8,128)} %copy.8) | copy-start | bytes 1572868
  174.9 1.8 %copy-start.2 = (f32[512,128]{1,0:T(8,128)}, f32[512,128]{1,0:T(8,128)S(1)}, u32[]{:S(2)}) copy-start(f32[512,128]{1,0:T(8,128)S(1)} %fusion.1) | copy-start | bytes 786436
where the time goes:
time: 180 us
  blocking collectives  104 us (58%)
  waiting for transfers between devices  29.9 us (17%)
  Pallas kernels  22.9 us (13%)
  matrix products  10.1 us (6%)
  local copies, waits for them, and re-layouts  6.91 us (4%)
  starting transfers between devices  5.11 us (3%)
    all_to_all x1, blocking collectives, sent_to_all(): lax.all_to_all(jnp.broadcast_to(x[None], (size, *x.shape)), axis, 0, 0, t...  62.3 us
    all_to_all x1, blocking collectives, summed(): lax.all_to_all(x.reshape(size, rows, x.shape[1]), axis, 0, 0, tiled=True)  41.9 us
    all_to_all x1, waiting for transfers between devices, sent_to_all(): lax.all_to_all(jnp.broadcast_to(x[None], (size, *x.shape)), axis, 0, 0, t...  29.9 us
    pallas_call x1, Pallas kernels, factor(): pl.pallas_call(factor_kernel, out_shape=(out, out), scratch_shapes=[pltpu...  22.9 us
    all_to_all x1, starting transfers between devices, sent_to_all(): lax.all_to_all(jnp.broadcast_to(x[None], (size, *x.shape)), axis, 0, 0, t...  5.11 us
  transfers between devices with their start and end apart: 1, of which 1 were waited for; matrix products, arithmetic and copies ran while one was open for 1% of the time, Pallas kernels for 0%

commit v1 on v0

--- a/solution.py
+++ b/solution.py
@@ -10,6 +10,9 @@
 V = 8
 NB = N // B
 NP = B // V
+X = 4
+Z = 8
+SHARE_ROWS = B // X
 HI = lax.Precision.HIGHEST
 F32 = jnp.float32
 
@@ -63,8 +66,18 @@
     return lax.dot_general(a, b, (dims, ((), ())), precision=HI, preferred_element_type=F32)
 
 
-def factor_kernel(g_ref, r_ref, w_ref, m_ref):
-    m_ref[...] = g_ref[...]
+def tile(g_ref, block, t):
+    s = block * SHARE_ROWS + (t % 4) * V
+    return g_ref[s // 40 * 4 + t // 4, s % 40 : s % 40 + V, :]
+
+
+def factor_kernel(g_ref, r_ref, w_ref, end_ref, m_ref):
+    block = 0
+    for i in range(NB):
+        for j in range(i, NB):
+            for t in range(NP):
+                m_ref[i * B + V * t : i * B + V * (t + 1), j * B : (j + 1) * B] = tile(g_ref, block, t)
+            block += 1
     r_ref[...] = jnp.zeros_like(r_ref)
     for k in range(NB):
         o = k * B
@@ -78,48 +91,114 @@
             w_ref[o:e, e:] = jnp.zeros((B, N - e), F32)
             ps = mm(v, m_ref[o:e, e:])
             r_ref[o:e, e:] = ps
-            lt = mm(m_ref[e:, o:e], v, ((1,), (1,)))
-            m_ref[e:, e:] = m_ref[e:, e:] - mm(lt, ps)
-            if k:
-                m_ref[e:, :o] = m_ref[e:, :o] - mm(lt, w_ref[o:e, :o])
-            m_ref[e:, o:e] = -mm(lt, v)
-
-
-def factor(gram):
+            for i in range(k + 1, NB):
+                q, lt = i * B, ps[:, (i - k - 1) * B : (i - k) * B].T
+                m_ref[q : q + B, q:] = m_ref[q : q + B, q:] - mm(lt, ps[:, q - e :])
+                if k:
+                    m_ref[q : q + B, :o] = m_ref[q : q + B, :o] - mm(lt, w_ref[o:e, :o])
+                m_ref[q : q + B, o:e] = -mm(lt, v)
+    end_ref[...] = jnp.zeros_like(end_ref)
+
+
+def factor(shares):
     out = jax.ShapeDtypeStruct((N, N), F32)
     vmem = pl.BlockSpec(memory_space=pltpu.VMEM)
     return pl.pallas_call(
         factor_kernel,
-        out_shape=(out, out),
+        out_shape=(out, out, jax.ShapeDtypeStruct((V, B), F32)),
         scratch_shapes=[pltpu.VMEM((N, N), F32)],
         in_specs=[vmem],
+        out_specs=(vmem, vmem, vmem),
+        compiler_params=pltpu.CompilerParams(vmem_limit_bytes=32 * 2**20),
+        cost_estimate=pl.CostEstimate(flops=20_000_000_000, bytes_accessed=3 * 2**20, transcendentals=0),
+        name="factor",
+    )(shares)
+
+
+def sent_to_all(x, axis, groups=None):
+    size = len(groups[0]) if groups else lax.axis_size(axis)
+    copies = jnp.broadcast_to(x[None], (size, *x.shape))
+    return lax.all_to_all(copies, axis, 0, 0, axis_index_groups=groups, tiled=True)
+
+
+def swapped(x):
+    return lax.ppermute(x, "half", [(0, 1), (1, 0)])
+
+
+def gram_kernel(p_ref, own_ref, g_ref):
+    first = lax.axis_index("dev") % X * SHARE_ROWS
+    block = 0
+    for i in range(NB):
+        g_ref[:, i * B :] = mm(p_ref[:, i * B : (i + 1) * B], p_ref[:, i * B :], ((0,), (0,)))
+        for j in range(i, NB):
+            for t in range(SHARE_ROWS // V):
+                s = block * SHARE_ROWS + t * V
+                row = pl.multiple_of(first + t * V, V)
+                own_ref[s // 40, s % 40 : s % 40 + V, :] = g_ref[pl.ds(row, V), j * B : (j + 1) * B]
+            block += 1
+
+
+def gram_shares(rows):
+    vmem = pl.BlockSpec(memory_space=pltpu.VMEM)
+    return pl.pallas_call(
+        gram_kernel,
+        out_shape=jax.ShapeDtypeStruct((Z, 40, B), F32),
+        scratch_shapes=[pltpu.VMEM((B, N), F32)],
+        in_specs=[vmem],
+        out_specs=vmem,
+        name="gram",
+    )(rows)
+
+
+def finish_kernel(w_ref, kept_ref, other_ref, p_ref, t_ref, y_ref, r_ref):
+    first = lax.axis_index("half") == 0
+    kept, other = kept_ref[...], other_ref[...]
+    cross = jnp.concatenate([jnp.where(first, kept, other), jnp.where(first, other, kept)], 0)
+    projected = mm(w_ref[...], cross)
+    y_ref[...] = projected
+    solved = mm(w_ref[...], projected, ((0,), (0,)))
+    r_ref[...] = t_ref[...] - mm(p_ref[...], solved)
+
+
+def finish(inverse, kept, other, panel_group, trailing):
+    vmem = pl.BlockSpec(memory_space=pltpu.VMEM)
+    return pl.pallas_call(
+        finish_kernel,
+        out_shape=(
+            jax.ShapeDtypeStruct((N, trailing.shape[1]), F32),
+            jax.ShapeDtypeStruct(trailing.shape, F32),
+        ),
+        in_specs=[vmem] * 5,
         out_specs=(vmem, vmem),
         compiler_params=pltpu.CompilerParams(vmem_limit_bytes=32 * 2**20),
-        name="factor",
-    )(gram)
-
-
-def sent_to_all(x, axis):
-    size = lax.axis_size(axis)
-    return lax.all_to_all(jnp.broadcast_to(x[None], (size, *x.shape)), axis, 0, 0, tiled=True)
-
-
-def summed(x, axis):
-    size = lax.axis_size(axis)
-    rows = x.shape[0] // size
-    share = lax.all_to_all(x.reshape(size, rows, x.shape[1]), axis, 0, 0, tiled=True).sum(0)
-    return sent_to_all(share, axis).reshape(x.shape)
+        name="finish",
+    )(inverse, kept, other, panel_group, trailing)
 
 
 def on_device(panel_block, trailing):
-    panel_group = sent_to_all(panel_block, "dev").reshape(-1, N)
-    gram_part = jnp.dot(panel_group.T, panel_group, precision=HI)
-    cross_part = jnp.dot(panel_group.T, trailing, precision=HI)
-    total = summed(jnp.concatenate([gram_part, cross_part], 1), ("half", "grp"))
-    triangle, inverse = factor(total[:, :N])
-    projected = jnp.dot(inverse, total[:, N:], precision=HI)
-    solved = jnp.dot(inverse.T, projected, precision=HI)
-    remainder = trailing - jnp.dot(panel_group, solved, precision=HI)
+    along_x = [[z * X + x for x in range(X)] for z in range(Z)]
+    along_z = [[z * X + x for z in range(Z)] for x in range(X)]
+    half = lax.axis_index("half")
+    rows = sent_to_all(panel_block, "dev", along_x).reshape(-1, N)
+    panel_group = lax.all_gather(rows, "dev", axis=0, axis_index_groups=along_z, tiled=True)
+
+    own = gram_shares(rows)
+    share = lax.all_to_all(own, "dev", 0, 0, axis_index_groups=along_z, tiled=True).sum(0)
+    share = share + swapped(share)
+    share = sent_to_all(share, "grp").sum(0)
+    shares = sent_to_all(share, "dev")
+    panel_group, _ = lax.optimization_barrier((panel_group, share))
+
+    cross = mm(panel_group, trailing, ((0,), (0,))).reshape(2, N // 2, -1)
+    kept = lax.dynamic_index_in_dim(cross, half, 0, keepdims=False)
+    given = lax.dynamic_index_in_dim(cross, 1 - half, 0, keepdims=False)
+    kept = kept + swapped(given)
+    shares, kept = lax.optimization_barrier((shares, kept))
+    triangle, inverse, end = factor(shares)
+    kept = sent_to_all(kept, "grp").sum(0)
+    kept, _ = lax.optimization_barrier((kept, end))
+    other = swapped(kept)
+    projected, remainder = finish(inverse, kept, other, panel_group, trailing)
     return (triangle, projected, remainder)
 
 

time: 180 us -> 155 us (0.86)
  blocking collectives: 104 us -> 72.9 us
  waiting for transfers between devices: 29.9 us -> 8.84 us
  starting transfers between devices: 5.11 us -> 20.9 us
  between operations: 0.74 us -> 14.1 us
  Pallas kernels: 22.9 us -> 30.6 us
  matrix products: 10.1 us -> 5.01 us
  local copies, waits for them, and re-layouts: 6.91 us -> 1.85 us
    all_to_all x2 -> x4, blocking collectives: 104 us -> 72.9 us  [the longest x3 54.4 us: sent_to_all(): lax.all_to_all(copies, axis, 0, 0, axis_index_groups=groups, tiled=True)]
    all_to_all x1, waiting for transfers between devices: 29.9 us -> 7.02 us  [sent_to_all(): lax.all_to_all(copies, axis, 0, 0, axis_index_groups=groups, tiled=True)]
    ppermute x0 -> x3, starting transfers between devices: none -> 17 us  [swapped(): return lax.ppermute(x, 'half', [(0, 1), (1, 0)])]
    pallas_call x1 -> x3, Pallas kernels: 22.9 us -> 30.6 us  [the longest x1 22.1 us: factor(): pl.pallas_call(factor_kernel, out_shape=(out, out, jax.ShapeDtypeStruct((...]
    dot_general x5 -> x1, matrix products: 10.1 us -> 5.01 us  [mm(): lax.dot_general(a, b, (dims, ((), ())), precision=HI, preferred_element_t...]
    unnamed x8 -> x4, local copies, waits for them, and re-layouts: 3.05 us -> 0.01 us
  transfers between devices with their start and end apart: 1 -> 5, of which waited for: 1 -> 3; matrix products, arithmetic and copies ran while one was open for 1% -> 4% of each run, Pallas kernels for 0% -> 16%
where the time goes in v1:
time: 155 us; the launch traced here: 154 us
  blocking collectives  72.9 us (47%)
  Pallas kernels  30.6 us (20%)
  starting transfers between devices  20.9 us (13%)
  between operations  14.1 us (9%)
  waiting for transfers between devices  8.84 us (6%)
  matrix products  5.01 us (3%)
  local copies, waits for them, and re-layouts  1.85 us (1%)
    all_to_all x3, blocking collectives, sent_to_all(): lax.all_to_all(copies, axis, 0, 0, axis_index_groups=groups, tiled=True)  54.4 us
    pallas_call x1, Pallas kernels, factor(): pl.pallas_call(factor_kernel, out_shape=(out, out, jax.ShapeDtypeStruct((...  22.1 us
    all_to_all x1, blocking collectives, on_device(): lax.all_to_all(own, 'dev', 0, 0, axis_index_groups=along_z, tiled=True)  18.4 us
    ppermute x3, starting transfers between devices, swapped(): return lax.ppermute(x, 'half', [(0, 1), (1, 0)])  17 us
    all_to_all x1, waiting for transfers between devices, sent_to_all(): lax.all_to_all(copies, axis, 0, 0, axis_index_groups=groups, tiled=True)  7.02 us
    pallas_call x1, Pallas kernels, finish(): pl.pallas_call(finish_kernel, out_shape=(jax.ShapeDtypeStruct((N, trailin...  6.01 us
    dot_general x1, matrix products, mm(): lax.dot_general(a, b, (dims, ((), ())), precision=HI, preferred_element_t...  5.01 us
    all_to_all x1, starting transfers between devices, sent_to_all(): lax.all_to_all(copies, axis, 0, 0, axis_index_groups=groups, tiled=True)  3.9 us
  transfers between devices with their start and end apart: 5, of which 3 were waited for; matrix products, arithmetic and copies ran while one was open for 4% of the time, Pallas kernels for 16%

profile of v1, /device:TPU:1, one launch (start us, length us, event | category | flops | bytes accessed | tf_op | source)
XLA Modules:
  0.0 154.3 jit_solution(15948470967251897083)
XLA Ops:
  7.2 0.0 all-gather.2.cloned.1.call-start
  7.2 0.9 broadcast_in_dim.8
  8.1 10.3 %all_to_all.25 = f32[4,32,512]{2,1,0:T(8,128)} all-to-all(f32[4,32,512]{2,1,0:T(8,128)S(1)} %broadcast_in_dim.8), channel_id=1, replica_groups={{0,1,2,3},{4,5,6,7},{8,9,10,11},{12,13,14,15},{16,17,18,19},{20,21,22,2..., dimensions={0} | all-to-all | bytes 524288 | tf_op jit(solution)/shard_map/all_to_all | solution.py:121
  18.4 0.0 copy-start.1
  18.4 0.0 all-gather.2.cloned.1.call-update
  18.4 2.4 %gram.1 = f32[8,40,128]{2,1,0:T(8,128)} custom-call(f32[128,512]{1,0:T(8,128)} %bitcast.9), custom_call_target="tpu_custom_call" | custom-call | tf_op jit(solution)/shard_map/gram/pallas_call | solution.py:143
  20.8 18.4 %all_to_all.26 = f32[8,40,128]{2,1,0:T(8,128)S(1)} all-to-all(f32[8,40,128]{2,1,0:T(8,128)} %gram.1), channel_id=1, replica_groups={{0,4,8,12,16,20,24,28},{1,5,9,13,17,21,25,29},{2,6,10,14,18,22,26,30},{..., dimensions={0} | all-to-all | bytes 327680 | tf_op jit(solution)/shard_map/all_to_all | solution.py:186
  39.3 5.4 %collective-permute-start = (f32[40,128]{1,0:T(8,128)S(1)}, f32[40,128]{1,0:T(8,128)S(1)}, u32[]{:S(2)}, u32[]{:S(2)}) collective-permute-start(f32[40,128]{1,0:T(8,128)S(1)} %reduce_sum.27), channel_id=1, source_target_pairs={{0,256},{256,0},{1,257},{257,1},{2,258},{258,2},{3,259},{259,3},{4... | collective-permute-start | bytes 61448 | tf_op jit(solution)/shard_map/ppermute | solution.py:125
  44.7 0.8 collective-permute-done
  45.5 15.3 %all_to_all.27 = f32[8,40,128]{2,1,0:T(8,128)S(1)} all-to-all(f32[8,40,128]{2,1,0:T(8,128)S(1)} %broadcast_in_dim.9), channel_id=1, replica_groups=mesh['half'=2,'grp'=8,'dev'=32] {'grp'}, dimensions={0} | all-to-all | bytes 327680 | tf_op jit(solution)/shard_map/all_to_all | solution.py:121
  60.8 0.9 broadcast_in_dim.10
  61.7 3.9 %all-to-all-start.3 = ((f32[32,40,128]{2,1,0:T(8,128)}), f32[32,40,128]{2,1,0:T(8,128)S(1)}, u32[]{:S(2)}, u32[]{:S(2)}) async-start(f32[32,40,128]{2,1,0:T(8,128)} %broadcast_in_dim.10), calls=%async_computation.3 | async-start | bytes 1310720 | tf_op jit(solution)/shard_map/all_to_all | solution.py:121
  65.6 0.0 all-gather.2.cloned.1.call-done.p_ref
  65.6 0.0 copy-done.1
  65.7 5.0 %fusion = f32[512,128]{1,0:T(8,128)S(1)} fusion(f32[1024,512]{1,0:T(8,128)} %all-gather.2.cloned.1.call-done.p_ref, f32[1024,128]{1,0:T(8,128)S(1)} %copy-done.1), kind=kOutput, calls=%fused_computation.2 | convolution fusion | flops 805306368 | bytes 2883584 | tf_op jit(solution)/shard_map/dot_general | solution.py:66
  70.7 4.6 %collective-permute-start.1 = (f32[256,128]{1,0:T(8,128)S(1)}, f32[256,128]{1,0:T(8,128)S(1)}, u32[]{:S(2)}, u32[]{:S(2)}) collective-permute-start(f32[256,128]{1,0:T(8,128)S(1)} %dynamic-slice_bitcast_fusion), channel_id=1, source_target_pairs={{0,256},{256,0},{1,257},{257,1},{2,258},{258,2},{3,259},{259,3},{4... | collective-permute-start | bytes 393224 | tf_op jit(solution)/shard_map/ppermute | solution.py:125
  75.3 1.0 collective-permute-done.1
  76.3 7.0 %all-to-all-done.3.g_ref = f32[32,40,128]{2,1,0:T(8,128)S(1)} async-done(((f32[32,40,128]{2,1,0:T(8,128)}), f32[32,40,128]{2,1,0:T(8,128)S(1)}, u32[]{:S(2)}, u32[]{:S(2)}) %all-to-all-start.3) | async-done | bytes 655392 | tf_op jit(solution)/shard_map/all_to_all | solution.py:121
  83.3 0.1 broadcast_in_dim.11
  83.3 28.9 %all_to_all.28 = f32[8,256,128]{2,1,0:T(8,128)S(1)} all-to-all(f32[8,256,128]{2,1,0:T(8,128)S(1)} %broadcast_in_dim.11), channel_id=1, replica_groups=mesh['half'=2,'grp'=8,'dev'=32] {'grp'}, dimensions={0} | all-to-all | bytes 2097152 | tf_op jit(solution)/shard_map/all_to_all | solution.py:121
  112.2 0.1 reduce_sum.29.kept_ref
  112.3 0.0 copy-start
  112.3 7.0 %collective-permute-start.2 = (f32[256,128]{1,0:T(8,128)S(1)}, f32[256,128]{1,0:T(8,128)S(1)}, u32[]{:S(2)}, u32[]{:S(2)}) collective-permute-start(f32[256,128]{1,0:T(8,128)S(1)} %reduce_sum.29.kept_ref), channel_id=1, source_target_pairs={{0,256},{256,0},{1,257},{257,1},{2,258},{258,2},{3,259},{259,3},{4... | collective-permute-start | bytes 393224 | tf_op jit(solution)/shard_map/ppermute | solution.py:125
  119.3 22.1 %factor.1 = (f32[512,512]{1,0:T(8,128)}, f32[512,512]{1,0:T(8,128)S(1)}, f32[8,128]{1,0:T(8,128)}) custom-call(f32[32,40,128]{2,1,0:T(8,128)S(1)} %all-to-all-done.3.g_ref), custom_call_target="tpu_custom_call" | custom-call | flops 20000000000 | bytes 3145728 | tf_op jit(solution)/shard_map/factor/pallas_call | solution.py:106
  141.4 0.0 collective-permute-done.2.other_ref
  141.4 0.0 copy-done
  141.4 6.0 %finish.1 = (f32[512,128]{1,0:T(8,128)}, f32[1024,128]{1,0:T(8,128)}) custom-call(f32[512,512]{1,0:T(8,128)S(1)} %get-tuple-element.13.w_ref, f32[256,128]{1,0:T(8,128)S(1)} %reduce_sum.29.kept_ref, f32[256,128]{1,0:T(8,128)S(1)} %collective-permute-done.2.other_ref, f32[1024,512]{1,0:T(8,128)S(1)} %copy-done, f32[1024,128]{1,0:T(8,128)S(1)} %copy-done.1), custom_call_target="tpu_custom_call" | custom-call | tf_op jit(solution)/shard_map/finish/pallas_call | solution.py:165
  (6 shorter events, 0.1 us)
Async XLA Ops:
  7.2 58.5 %all-gather.2.cloned.1.call-start = ((), (), s32[]{:S(2)}) async-start(), calls=%async_computation.5 | async-start | bytes 2359296 | tf_op jit(solution)/shard_map/all_gather | solution.py:183
  18.4 47.3 %copy-start.1 = (f32[1024,128]{1,0:T(8,128)S(1)}, f32[1024,128]{1,0:T(8,128)}, u32[]{:S(2)}) copy-start(f32[1024,128]{1,0:T(8,128)} %t_ref.1) | copy-start | bytes 1572868
  39.3 6.2 %collective-permute-start = (f32[40,128]{1,0:T(8,128)S(1)}, f32[40,128]{1,0:T(8,128)S(1)}, u32[]{:S(2)}, u32[]{:S(2)}) collective-permute-start(f32[40,128]{1,0:T(8,128)S(1)} %reduce_sum.27), channel_id=1, source_target_pairs={{0,256},{256,0},{1,257},{257,1},{2,258},{258,2},{3,259},{259,3},{4... | collective-permute-start | bytes 61448 | tf_op jit(solution)/shard_map/ppermute | solution.py:125
  61.7 21.6 %all-to-all-start.3 = ((f32[32,40,128]{2,1,0:T(8,128)}), f32[32,40,128]{2,1,0:T(8,128)S(1)}, u32[]{:S(2)}, u32[]{:S(2)}) async-start(f32[32,40,128]{2,1,0:T(8,128)} %broadcast_in_dim.10), calls=%async_computation.3 | async-start | bytes 1310720 | tf_op jit(solution)/shard_map/all_to_all | solution.py:121
  70.7 5.5 %collective-permute-start.1 = (f32[256,128]{1,0:T(8,128)S(1)}, f32[256,128]{1,0:T(8,128)S(1)}, u32[]{:S(2)}, u32[]{:S(2)}) collective-permute-start(f32[256,128]{1,0:T(8,128)S(1)} %dynamic-slice_bitcast_fusion), channel_id=1, source_target_pairs={{0,256},{256,0},{1,257},{257,1},{2,258},{258,2},{3,259},{259,3},{4... | collective-permute-start | bytes 393224 | tf_op jit(solution)/shard_map/ppermute | solution.py:125
  112.3 29.2 %copy-start = (f32[1024,512]{1,0:T(8,128)S(1)}, f32[1024,512]{1,0:T(8,128)}, u32[]{:S(2)}) copy-start(f32[1024,512]{1,0:T(8,128)} %all-gather.2.cloned.1.call-done.p_ref) | copy-start | bytes 6291460
  112.3 29.1 %collective-permute-start.2 = (f32[256,128]{1,0:T(8,128)S(1)}, f32[256,128]{1,0:T(8,128)S(1)}, u32[]{:S(2)}, u32[]{:S(2)}) collective-permute-start(f32[256,128]{1,0:T(8,128)S(1)} %reduce_sum.29.kept_ref), channel_id=1, source_target_pairs={{0,256},{256,0},{1,257},{257,1},{2,258},{258,2},{3,259},{259,3},{4... | collective-permute-start | bytes 393224 | tf_op jit(solution)/shard_map/ppermute | solution.py:125
Sparse Core Ops, SparseCore 0:
  18.5 44.7 all-gather.1

commit v2 on v1

--- a/solution.py
+++ b/solution.py
@@ -12,7 +12,8 @@
 NP = B // V
 X = 4
 Z = 8
-SHARE_ROWS = B // X
+ROWS = 32
+SHARE_ROWS = B // Z
 HI = lax.Precision.HIGHEST
 F32 = jnp.float32
 
@@ -67,11 +68,11 @@
 
 
 def tile(g_ref, block, t):
-    s = block * SHARE_ROWS + (t % 4) * V
-    return g_ref[s // 40 * 4 + t // 4, s % 40 : s % 40 + V, :]
-
-
-def factor_kernel(g_ref, r_ref, w_ref, end_ref, m_ref):
+    s = block * SHARE_ROWS + (t % 2) * V
+    return g_ref[t // 2 * X + s // 40, s % 40 : s % 40 + V, :]
+
+
+def factor_kernel(g_ref, r_ref, w_ref, m_ref):
     block = 0
     for i in range(NB):
         for j in range(i, NB):
@@ -97,7 +98,6 @@
                 if k:
                     m_ref[q : q + B, :o] = m_ref[q : q + B, :o] - mm(lt, w_ref[o:e, :o])
                 m_ref[q : q + B, o:e] = -mm(lt, v)
-    end_ref[...] = jnp.zeros_like(end_ref)
 
 
 def factor(shares):
@@ -105,10 +105,10 @@
     vmem = pl.BlockSpec(memory_space=pltpu.VMEM)
     return pl.pallas_call(
         factor_kernel,
-        out_shape=(out, out, jax.ShapeDtypeStruct((V, B), F32)),
+        out_shape=(out, out),
         scratch_shapes=[pltpu.VMEM((N, N), F32)],
         in_specs=[vmem],
-        out_specs=(vmem, vmem, vmem),
+        out_specs=(vmem, vmem),
         compiler_params=pltpu.CompilerParams(vmem_limit_bytes=32 * 2**20),
         cost_estimate=pl.CostEstimate(flops=20_000_000_000, bytes_accessed=3 * 2**20, transcendentals=0),
         name="factor",
@@ -125,80 +125,121 @@
     return lax.ppermute(x, "half", [(0, 1), (1, 0)])
 
 
-def gram_kernel(p_ref, own_ref, g_ref):
-    first = lax.axis_index("dev") % X * SHARE_ROWS
+VMEM = pl.BlockSpec(memory_space=pltpu.VMEM)
+PARAMS = pltpu.CompilerParams(vmem_limit_bytes=32 * 2**20)
+
+
+def gram_kernel(p_ref, own_ref, t_ref):
+    first = lax.axis_index("dev") // X * SHARE_ROWS
+    for i in range(NB):
+        t_ref[i * B : (i + 1) * B, :] = p_ref[:, i * B : (i + 1) * B].T
+    left = jnp.concatenate([t_ref[pl.ds(pl.multiple_of(i * B + first, SHARE_ROWS), SHARE_ROWS), :] for i in range(NB)], 0)
+    g = mm(left, p_ref[...])
     block = 0
     for i in range(NB):
-        g_ref[:, i * B :] = mm(p_ref[:, i * B : (i + 1) * B], p_ref[:, i * B :], ((0,), (0,)))
         for j in range(i, NB):
             for t in range(SHARE_ROWS // V):
-                s = block * SHARE_ROWS + t * V
-                row = pl.multiple_of(first + t * V, V)
-                own_ref[s // 40, s % 40 : s % 40 + V, :] = g_ref[pl.ds(row, V), j * B : (j + 1) * B]
+                s, row = block * SHARE_ROWS + t * V, i * SHARE_ROWS + t * V
+                own_ref[s // 40, s % 40 : s % 40 + V, :] = g[row : row + V, j * B : (j + 1) * B]
             block += 1
 
 
 def gram_shares(rows):
-    vmem = pl.BlockSpec(memory_space=pltpu.VMEM)
     return pl.pallas_call(
         gram_kernel,
-        out_shape=jax.ShapeDtypeStruct((Z, 40, B), F32),
-        scratch_shapes=[pltpu.VMEM((B, N), F32)],
-        in_specs=[vmem],
-        out_specs=vmem,
+        out_shape=jax.ShapeDtypeStruct((X, 40, B), F32),
+        scratch_shapes=[pltpu.VMEM((N, rows.shape[0]), F32)],
+        in_specs=[VMEM],
+        out_specs=VMEM,
+        compiler_params=PARAMS,
         name="gram",
     )(rows)
 
 
-def finish_kernel(w_ref, kept_ref, other_ref, p_ref, t_ref, y_ref, r_ref):
+def slab_rows(k, z):
+    x = (lax.axis_index("dev") + (X - k)) % X
+    return pl.ds(pl.multiple_of((z * X + x) * ROWS, ROWS), ROWS)
+
+
+def cross_kernel(p0, p1, p2, p3, t_ref, kept_ref, given_ref):
+    total = None
+    for k, p_ref in enumerate((p0, p1, p2, p3)):
+        t = jnp.concatenate([t_ref[slab_rows(k, z), :] for z in range(Z)], 0)
+        part = mm(t.T, p_ref[...])
+        total = part if total is None else total + part
+    first = lax.axis_index("half") == 0
+    low, high = total[:, : N // 2], total[:, N // 2 :]
+    kept_ref[...] = jnp.where(first, low, high)
+    given_ref[...] = jnp.where(first, high, low)
+
+
+def cross_halves(blocks, trailing):
+    out = jax.ShapeDtypeStruct((trailing.shape[1], N // 2), F32)
+    return pl.pallas_call(
+        cross_kernel,
+        out_shape=(out, out),
+        in_specs=[VMEM] * 5,
+        out_specs=(VMEM, VMEM),
+        compiler_params=PARAMS,
+        cost_estimate=pl.CostEstimate(flops=2_000_000_000, bytes_accessed=3 * 2**20, transcendentals=0),
+        name="cross",
+    )(*blocks, trailing)
+
+
+def finish_kernel(w_ref, kept_ref, other_ref, p0, p1, p2, p3, t_ref, y_ref, r_ref):
     first = lax.axis_index("half") == 0
     kept, other = kept_ref[...], other_ref[...]
-    cross = jnp.concatenate([jnp.where(first, kept, other), jnp.where(first, other, kept)], 0)
-    projected = mm(w_ref[...], cross)
-    y_ref[...] = projected
-    solved = mm(w_ref[...], projected, ((0,), (0,)))
-    r_ref[...] = t_ref[...] - mm(p_ref[...], solved)
-
-
-def finish(inverse, kept, other, panel_group, trailing):
-    vmem = pl.BlockSpec(memory_space=pltpu.VMEM)
+    cross = jnp.concatenate([jnp.where(first, kept, other), jnp.where(first, other, kept)], 1)
+    projected = mm(cross, w_ref[...], ((1,), (1,)))
+    y_ref[...] = projected.T
+    solved = mm(projected, w_ref[...])
+    for k, p_ref in enumerate((p0, p1, p2, p3)):
+        part = mm(p_ref[...], solved, ((1,), (1,)))
+        for z in range(Z):
+            here = slab_rows(k, z)
+            r_ref[here, :] = t_ref[here, :] - part[z * ROWS : (z + 1) * ROWS, :]
+
+
+def finish(inverse, kept, other, blocks, trailing):
     return pl.pallas_call(
         finish_kernel,
         out_shape=(
             jax.ShapeDtypeStruct((N, trailing.shape[1]), F32),
             jax.ShapeDtypeStruct(trailing.shape, F32),
         ),
-        in_specs=[vmem] * 5,
-        out_specs=(vmem, vmem),
-        compiler_params=pltpu.CompilerParams(vmem_limit_bytes=32 * 2**20),
+        in_specs=[VMEM] * 8,
+        out_specs=(VMEM, VMEM),
+        compiler_params=PARAMS,
         name="finish",
-    )(inverse, kept, other, panel_group, trailing)
+    )(inverse, kept, other, *blocks, trailing)
 
 
 def on_device(panel_block, trailing):
     along_x = [[z * X + x for x in range(X)] for z in range(Z)]
     along_z = [[z * X + x for z in range(Z)] for x in range(X)]
-    half = lax.axis_index("half")
-    rows = sent_to_all(panel_block, "dev", along_x).reshape(-1, N)
-    panel_group = lax.all_gather(rows, "dev", axis=0, axis_index_groups=along_z, tiled=True)
+    rows = sent_to_all(panel_block, "dev", along_z).reshape(-1, N)
 
     own = gram_shares(rows)
-    share = lax.all_to_all(own, "dev", 0, 0, axis_index_groups=along_z, tiled=True).sum(0)
+    share = lax.all_to_all(own, "dev", 0, 0, axis_index_groups=along_x, tiled=True).sum(0)
+    rows, _ = lax.optimization_barrier((rows, own))
+    blocks = [rows]
+    for k in range(1, X):
+        moves = [(z * X + x, z * X + (x + k) % X) for z in range(Z) for x in range(X)]
+        blocks.append(lax.ppermute(rows, "dev", moves))
     share = share + swapped(share)
     share = sent_to_all(share, "grp").sum(0)
     shares = sent_to_all(share, "dev")
-    panel_group, _ = lax.optimization_barrier((panel_group, share))
-
-    cross = mm(panel_group, trailing, ((0,), (0,))).reshape(2, N // 2, -1)
-    kept = lax.dynamic_index_in_dim(cross, half, 0, keepdims=False)
-    given = lax.dynamic_index_in_dim(cross, 1 - half, 0, keepdims=False)
+
+    kept, given = cross_halves(blocks, trailing)
     kept = kept + swapped(given)
-    shares, kept = lax.optimization_barrier((shares, kept))
-    triangle, inverse, end = factor(shares)
-    kept = sent_to_all(kept, "grp").sum(0)
-    kept, _ = lax.optimization_barrier((kept, end))
+    groups = lax.axis_size("grp")
+    kept, _ = lax.optimization_barrier((kept, share))
+    parts = [lax.ppermute(kept, "grp", [(g, (g + k) % groups) for g in range(groups)]) for k in (4, 3, 5, 2, 6, 1, 7)]
+    kept = sum(parts, kept)
     other = swapped(kept)
-    projected, remainder = finish(inverse, kept, other, panel_group, trailing)
+
+    triangle, inverse = factor(shares)
+    projected, remainder = finish(inverse, kept, other, blocks, trailing)
     return (triangle, projected, remainder)
 
 

time: 155 us -> 162 us (1.045)
  the two profiles are of different devices: /device:TPU:1 before, /device:TPU:17 now
where the time goes in v2:
time: 162 us
  starting transfers between devices  57.3 us (35%)
  waiting for transfers between devices  38.6 us (24%)
  blocking collectives  34.2 us (21%)
  Pallas kernels  28.2 us (17%)
  local copies, waits for them, and re-layouts  2.45 us (2%)
    ppermute x7, starting transfers between devices, on_device(): lax.ppermute(kept, 'grp', [(g, (g + k) % groups) for g in range(groups)])  26.2 us
    all_to_all x1, blocking collectives, sent_to_all(): lax.all_to_all(copies, axis, 0, 0, axis_index_groups=groups, tiled=True)  25.8 us
    ppermute x3, waiting for transfers between devices, on_device(): blocks.append(lax.ppermute(rows, 'dev', moves))  24.1 us
    pallas_call x1, Pallas kernels, factor(): pl.pallas_call(factor_kernel, out_shape=(out, out), scratch_shapes=[pltpu...  22.1 us
    ppermute x7, waiting for transfers between devices, on_device(): lax.ppermute(kept, 'grp', [(g, (g + k) % groups) for g in range(groups)])  12.6 us
    ppermute x3, starting transfers between devices, swapped(): return lax.ppermute(x, 'half', [(0, 1), (1, 0)])  11.7 us
    all_to_all x2, starting transfers between devices, sent_to_all(): lax.all_to_all(copies, axis, 0, 0, axis_index_groups=groups, tiled=True)  11.6 us
    all_to_all x1, blocking collectives, on_device(): lax.all_to_all(own, 'dev', 0, 0, axis_index_groups=along_x, tiled=True)  8.38 us
  transfers between devices with their start and end apart: 15, of which 7 were waited for; matrix products, arithmetic and copies ran while one was open for 1% of the time, Pallas kernels for 14%

profile of v2, /device:TPU:17, one launch (start us, length us, event | category | flops | bytes accessed | tf_op | source)
XLA Modules:
  0.0 161.7 jit_solution(14442109492362000053)
XLA Ops:
  0.6 0.9 broadcast_in_dim.6
  1.5 25.8 %all_to_all.20 = f32[8,32,512]{2,1,0:T(8,128)S(1)} all-to-all(f32[8,32,512]{2,1,0:T(8,128)S(1)} %broadcast_in_dim.6), channel_id=1, replica_groups={{0,4,8,12,16,20,24,28},{1,5,9,13,17,21,25,29},{2,6,10,14,18,22,26,30},{..., dimensions={0} | all-to-all | bytes 1048576 | tf_op jit(solution)/shard_map/all_to_all | solution.py:121
  27.4 0.6 gram.1
  27.9 8.4 %all_to_all.21 = f32[4,40,128]{2,1,0:T(8,128)S(1)} all-to-all(f32[4,40,128]{2,1,0:T(8,128)S(1)} %gram.1), channel_id=1, replica_groups={{0,1,2,3},{4,5,6,7},{8,9,10,11},{12,13,14,15},{16,17,18,19},{20,21,22,2..., dimensions={0} | all-to-all | bytes 163840 | tf_op jit(solution)/shard_map/all_to_all | solution.py:223
  36.3 5.8 %collective-permute-start = (f32[40,128]{1,0:T(8,128)S(1)}, f32[40,128]{1,0:T(8,128)S(1)}, u32[]{:S(2)}, u32[]{:S(2)}) collective-permute-start(f32[40,128]{1,0:T(8,128)S(1)} %reduce_sum.18), channel_id=1, source_target_pairs={{0,256},{256,0},{1,257},{257,1},{2,258},{258,2},{3,259},{259,3},{4... | collective-permute-start | bytes 61448 | tf_op jit(solution)/shard_map/ppermute | solution.py:125
  42.1 0.8 collective-permute-done
  43.0 0.7 broadcast_in_dim.7
  43.6 6.9 %all-to-all-start.2 = ((f32[8,40,128]{2,1,0:T(8,128)}), f32[8,40,128]{2,1,0:T(8,128)S(1)}, u32[]{:S(2)}, u32[]{:S(2)}) async-start(f32[8,40,128]{2,1,0:T(8,128)} %broadcast_in_dim.7), calls=%async_computation.2 | async-start | bytes 327680 | tf_op jit(solution)/shard_map/all_to_all | solution.py:121
  50.5 2.8 %collective-permute-start.3 = (f32[256,512]{1,0:T(8,128)S(1)}, f32[256,512]{1,0:T(8,128)S(1)}, u32[]{:S(2)}, u32[]{:S(2)}) collective-permute-start(f32[256,512]{1,0:T(8,128)S(1)} %bitcast.2), channel_id=1, source_target_pairs={{0,3},{1,0},{2,1},{3,2},{4,7},{5,4},{6,5},{7,6},{8,11},{9,8},{10,9... | collective-permute-start | bytes 1572872 | tf_op jit(solution)/shard_map/ppermute | solution.py:228
  53.3 3.1 %collective-permute-start.2 = (f32[256,512]{1,0:T(8,128)S(1)}, f32[256,512]{1,0:T(8,128)S(1)}, u32[]{:S(2)}, u32[]{:S(2)}) collective-permute-start(f32[256,512]{1,0:T(8,128)S(1)} %bitcast.3), channel_id=1, source_target_pairs={{0,2},{1,3},{2,0},{3,1},{4,6},{5,7},{6,4},{7,5},{8,10},{9,11},{10,... | collective-permute-start | bytes 1572872 | tf_op jit(solution)/shard_map/ppermute | solution.py:228
  56.4 1.9 %collective-permute-start.1 = (f32[256,512]{1,0:T(8,128)S(1)}, f32[256,512]{1,0:T(8,128)S(1)}, u32[]{:S(2)}, u32[]{:S(2)}) collective-permute-start(f32[256,512]{1,0:T(8,128)S(1)} %bitcast.4), channel_id=1, source_target_pairs={{0,1},{1,2},{2,3},{3,0},{4,5},{5,6},{6,7},{7,4},{8,9},{9,10},{10,1... | collective-permute-start | bytes 1572872 | tf_op jit(solution)/shard_map/ppermute | solution.py:228
  58.3 0.0 all-to-all-done.2
  58.4 0.9 broadcast_in_dim.8
  59.2 0.0 copy-start
  59.2 4.8 %all-to-all-start.3 = ((f32[32,40,128]{2,1,0:T(8,128)}), f32[32,40,128]{2,1,0:T(8,128)S(1)}, u32[]{:S(2)}, u32[]{:S(2)}) async-start(f32[32,40,128]{2,1,0:T(8,128)} %broadcast_in_dim.8), calls=%async_computation.3 | async-start | bytes 1310720 | tf_op jit(solution)/shard_map/all_to_all | solution.py:121
  64.0 0.9 collective-permute-done.3.p3
  64.9 4.1 %collective-permute-done.2.p2 = f32[256,512]{1,0:T(8,128)S(1)} collective-permute-done((f32[256,512]{1,0:T(8,128)S(1)}, f32[256,512]{1,0:T(8,128)S(1)}, u32[]{:S(2)}, u32[]{:S(2)}) %collective-permute-start.2) | collective-permute-done | bytes 524320 | tf_op jit(solution)/shard_map/ppermute | solution.py:228
  69.0 19.2 %collective-permute-done.1.p1 = f32[256,512]{1,0:T(8,128)S(1)} collective-permute-done((f32[256,512]{1,0:T(8,128)S(1)}, f32[256,512]{1,0:T(8,128)S(1)}, u32[]{:S(2)}, u32[]{:S(2)}) %collective-permute-start.1) | collective-permute-done | bytes 524320 | tf_op jit(solution)/shard_map/ppermute | solution.py:228
  88.1 0.0 copy-done
  88.1 1.2 cross.1
  89.3 2.5 %collective-permute-start.4 = (f32[128,256]{1,0:T(8,128)S(1)}, f32[128,256]{1,0:T(8,128)S(1)}, u32[]{:S(2)}, u32[]{:S(2)}) collective-permute-start(f32[128,256]{1,0:T(8,128)S(1)} %get-tuple-element.15), channel_id=1, source_target_pairs={{0,256},{256,0},{1,257},{257,1},{2,258},{258,2},{3,259},{259,3},{4... | collective-permute-start | bytes 393224 | tf_op jit(solution)/shard_map/ppermute | solution.py:125
  91.8 1.0 collective-permute-done.4
  92.8 2.2 %collective-permute-start.11 = (f32[128,256]{1,0:T(8,128)S(1)}, f32[128,256]{1,0:T(8,128)S(1)}, u32[]{:S(2)}, u32[]{:S(2)}) collective-permute-start(f32[128,256]{1,0:T(8,128)S(1)} %add.28), channel_id=1, source_target_pairs={{0,224},{32,0},{64,32},{96,64},{128,96},{160,128},{192,160},{224,1... | collective-permute-start | bytes 393224 | tf_op jit(solution)/shard_map/ppermute | solution.py:237
  95.0 3.1 %collective-permute-start.10 = (f32[128,256]{1,0:T(8,128)S(1)}, f32[128,256]{1,0:T(8,128)S(1)}, u32[]{:S(2)}, u32[]{:S(2)}) collective-permute-start(f32[128,256]{1,0:T(8,128)S(1)} %add.28), channel_id=1, source_target_pairs={{0,32},{32,64},{64,96},{96,128},{128,160},{160,192},{192,224},{224... | collective-permute-start | bytes 393224 | tf_op jit(solution)/shard_map/ppermute | solution.py:237
  98.1 3.1 %collective-permute-start.9 = (f32[128,256]{1,0:T(8,128)S(1)}, f32[128,256]{1,0:T(8,128)S(1)}, u32[]{:S(2)}, u32[]{:S(2)}) collective-permute-start(f32[128,256]{1,0:T(8,128)S(1)} %add.28), channel_id=1, source_target_pairs={{0,192},{32,224},{64,0},{96,32},{128,64},{160,96},{192,128},{224,1... | collective-permute-start | bytes 393224 | tf_op jit(solution)/shard_map/ppermute | solution.py:237
  101.2 4.3 %collective-permute-start.8 = (f32[128,256]{1,0:T(8,128)S(1)}, f32[128,256]{1,0:T(8,128)S(1)}, u32[]{:S(2)}, u32[]{:S(2)}) collective-permute-start(f32[128,256]{1,0:T(8,128)S(1)} %add.28), channel_id=1, source_target_pairs={{0,64},{32,96},{64,128},{96,160},{128,192},{160,224},{192,0},{224,... | collective-permute-start | bytes 393224 | tf_op jit(solution)/shard_map/ppermute | solution.py:237
  105.5 5.5 %collective-permute-start.7 = (f32[128,256]{1,0:T(8,128)S(1)}, f32[128,256]{1,0:T(8,128)S(1)}, u32[]{:S(2)}, u32[]{:S(2)}) collective-permute-start(f32[128,256]{1,0:T(8,128)S(1)} %add.28), channel_id=1, source_target_pairs={{0,160},{32,192},{64,224},{96,0},{128,32},{160,64},{192,96},{224,1... | collective-permute-start | bytes 393224 | tf_op jit(solution)/shard_map/ppermute | solution.py:237
  111.0 0.0 collective-permute-done.11
  111.0 2.8 %collective-permute-start.6 = (f32[128,256]{1,0:T(8,128)S(1)}, f32[128,256]{1,0:T(8,128)S(1)}, u32[]{:S(2)}, u32[]{:S(2)}) collective-permute-start(f32[128,256]{1,0:T(8,128)S(1)} %add.28), channel_id=1, source_target_pairs={{0,96},{32,128},{64,160},{96,192},{128,224},{160,0},{192,32},{224,... | collective-permute-start | bytes 393224 | tf_op jit(solution)/shard_map/ppermute | solution.py:237
  113.8 0.0 collective-permute-done.10
  113.8 5.2 %collective-permute-start.5 = (f32[128,256]{1,0:T(8,128)S(1)}, f32[128,256]{1,0:T(8,128)S(1)}, u32[]{:S(2)}, u32[]{:S(2)}) collective-permute-start(f32[128,256]{1,0:T(8,128)S(1)} %add.28), channel_id=1, source_target_pairs={{0,128},{32,160},{64,192},{96,224},{128,0},{160,32},{192,64},{224,... | collective-permute-start | bytes 393224 | tf_op jit(solution)/shard_map/ppermute | solution.py:237
  119.0 0.0 collective-permute-done.9
  119.1 0.0 collective-permute-done.8
  119.1 0.0 collective-permute-done.7
  119.1 6.2 %collective-permute-done.6 = f32[128,256]{1,0:T(8,128)S(1)} collective-permute-done((f32[128,256]{1,0:T(8,128)S(1)}, f32[128,256]{1,0:T(8,128)S(1)}, u32[]{:S(2)}, u32[]{:S(2)}) %collective-permute-start.6) | collective-permute-done | bytes 131104 | tf_op jit(solution)/shard_map/ppermute | solution.py:237
  125.2 6.5 %collective-permute-done.5 = f32[128,256]{1,0:T(8,128)S(1)} collective-permute-done((f32[128,256]{1,0:T(8,128)S(1)}, f32[128,256]{1,0:T(8,128)S(1)}, u32[]{:S(2)}, u32[]{:S(2)}) %collective-permute-start.5) | collective-permute-done | bytes 131104 | tf_op jit(solution)/shard_map/ppermute | solution.py:237
  131.7 0.1 add_add_fusion.kept_ref
  131.8 3.4 %collective-permute-start.12 = (f32[128,256]{1,0:T(8,128)S(1)}, f32[128,256]{1,0:T(8,128)S(1)}, u32[]{:S(2)}, u32[]{:S(2)}) collective-permute-start(f32[128,256]{1,0:T(8,128)S(1)} %add_add_fusion.kept_ref), channel_id=1, source_target_pairs={{0,256},{256,0},{1,257},{257,1},{2,258},{258,2},{3,259},{259,3},{4... | collective-permute-start | bytes 393224 | tf_op jit(solution)/shard_map/ppermute | solution.py:125
  135.2 0.0 all-to-all-done.3.g_ref
  135.2 22.1 %factor.1 = (f32[512,512]{1,0:T(8,128)}, f32[512,512]{1,0:T(8,128)S(1)}) custom-call(f32[32,40,128]{2,1,0:T(8,128)S(1)} %all-to-all-done.3.g_ref), custom_call_target="tpu_custom_call" | custom-call | flops 20000000000 | bytes 3145728 | tf_op jit(solution)/shard_map/factor/pallas_call | solution.py:106
  157.3 0.0 collective-permute-done.12.other_ref
  157.3 4.3 %finish.1 = (f32[512,128]{1,0:T(8,128)}, f32[1024,128]{1,0:T(8,128)}) custom-call(f32[512,512]{1,0:T(8,128)S(1)} %get-tuple-element.12.w_ref, f32[128,256]{1,0:T(8,128)S(1)} %add_add_fusion.kept_ref, f32[128,256]{1,0:T(8,128)S(1)} %collective-permute-done.12.other_ref, f32[256,512]{1,0:T(8,128)S(1)} %bitcast.6, f32[256,512]{1,0:T(8,128)S(1)} %collective-permute-done.1.p1, ...), custom_call_target="tpu_custom_call" | custom-call | tf_op jit(solution)/shard_map/finish/pallas_call | solution.py:204
  (4 shorter events, 0.0 us)
Async XLA Ops:
  36.3 6.6 %collective-permute-start = (f32[40,128]{1,0:T(8,128)S(1)}, f32[40,128]{1,0:T(8,128)S(1)}, u32[]{:S(2)}, u32[]{:S(2)}) collective-permute-start(f32[40,128]{1,0:T(8,128)S(1)} %reduce_sum.18), channel_id=1, source_target_pairs={{0,256},{256,0},{1,257},{257,1},{2,258},{258,2},{3,259},{259,3},{4... | collective-permute-start | bytes 61448 | tf_op jit(solution)/shard_map/ppermute | solution.py:125
  43.6 14.7 %all-to-all-start.2 = ((f32[8,40,128]{2,1,0:T(8,128)}), f32[8,40,128]{2,1,0:T(8,128)S(1)}, u32[]{:S(2)}, u32[]{:S(2)}) async-start(f32[8,40,128]{2,1,0:T(8,128)} %broadcast_in_dim.7), calls=%async_computation.2 | async-start | bytes 327680 | tf_op jit(solution)/shard_map/all_to_all | solution.py:121
  50.5 14.4 %collective-permute-start.3 = (f32[256,512]{1,0:T(8,128)S(1)}, f32[256,512]{1,0:T(8,128)S(1)}, u32[]{:S(2)}, u32[]{:S(2)}) collective-permute-start(f32[256,512]{1,0:T(8,128)S(1)} %bitcast.2), channel_id=1, source_target_pairs={{0,3},{1,0},{2,1},{3,2},{4,7},{5,4},{6,5},{7,6},{8,11},{9,8},{10,9... | collective-permute-start | bytes 1572872 | tf_op jit(solution)/shard_map/ppermute | solution.py:228
  53.3 15.7 %collective-permute-start.2 = (f32[256,512]{1,0:T(8,128)S(1)}, f32[256,512]{1,0:T(8,128)S(1)}, u32[]{:S(2)}, u32[]{:S(2)}) collective-permute-start(f32[256,512]{1,0:T(8,128)S(1)} %bitcast.3), channel_id=1, source_target_pairs={{0,2},{1,3},{2,0},{3,1},{4,6},{5,7},{6,4},{7,5},{8,10},{9,11},{10,... | collective-permute-start | bytes 1572872 | tf_op jit(solution)/shard_map/ppermute | solution.py:228
  56.4 31.7 %collective-permute-start.1 = (f32[256,512]{1,0:T(8,128)S(1)}, f32[256,512]{1,0:T(8,128)S(1)}, u32[]{:S(2)}, u32[]{:S(2)}) collective-permute-start(f32[256,512]{1,0:T(8,128)S(1)} %bitcast.4), channel_id=1, source_target_pairs={{0,1},{1,2},{2,3},{3,0},{4,5},{5,6},{6,7},{7,4},{8,9},{9,10},{10,1... | collective-permute-start | bytes 1572872 | tf_op jit(solution)/shard_map/ppermute | solution.py:228
  59.2 28.9 %copy-start = (f32[1024,128]{1,0:T(8,128)S(1)}, f32[1024,128]{1,0:T(8,128)}, u32[]{:S(2)}) copy-start(f32[1024,128]{1,0:T(8,128)} %t_ref.3) | copy-start | bytes 1572868
  59.2 75.9 %all-to-all-start.3 = ((f32[32,40,128]{2,1,0:T(8,128)}), f32[32,40,128]{2,1,0:T(8,128)S(1)}, u32[]{:S(2)}, u32[]{:S(2)}) async-start(f32[32,40,128]{2,1,0:T(8,128)} %broadcast_in_dim.8), calls=%async_computation.3 | async-start | bytes 1310720 | tf_op jit(solution)/shard_map/all_to_all | solution.py:121
  89.3 3.5 %collective-permute-start.4 = (f32[128,256]{1,0:T(8,128)S(1)}, f32[128,256]{1,0:T(8,128)S(1)}, u32[]{:S(2)}, u32[]{:S(2)}) collective-permute-start(f32[128,256]{1,0:T(8,128)S(1)} %get-tuple-element.15), channel_id=1, source_target_pairs={{0,256},{256,0},{1,257},{257,1},{2,258},{258,2},{3,259},{259,3},{4... | collective-permute-start | bytes 393224 | tf_op jit(solution)/shard_map/ppermute | solution.py:125
  92.8 18.2 %collective-permute-start.11 = (f32[128,256]{1,0:T(8,128)S(1)}, f32[128,256]{1,0:T(8,128)S(1)}, u32[]{:S(2)}, u32[]{:S(2)}) collective-permute-start(f32[128,256]{1,0:T(8,128)S(1)} %add.28), channel_id=1, source_target_pairs={{0,224},{32,0},{64,32},{96,64},{128,96},{160,128},{192,160},{224,1... | collective-permute-start | bytes 393224 | tf_op jit(solution)/shard_map/ppermute | solution.py:237
  95.0 18.8 %collective-permute-start.10 = (f32[128,256]{1,0:T(8,128)S(1)}, f32[128,256]{1,0:T(8,128)S(1)}, u32[]{:S(2)}, u32[]{:S(2)}) collective-permute-start(f32[128,256]{1,0:T(8,128)S(1)} %add.28), channel_id=1, source_target_pairs={{0,32},{32,64},{64,96},{96,128},{128,160},{160,192},{192,224},{224... | collective-permute-start | bytes 393224 | tf_op jit(solution)/shard_map/ppermute | solution.py:237
  98.1 20.9 %collective-permute-start.9 = (f32[128,256]{1,0:T(8,128)S(1)}, f32[128,256]{1,0:T(8,128)S(1)}, u32[]{:S(2)}, u32[]{:S(2)}) collective-permute-start(f32[128,256]{1,0:T(8,128)S(1)} %add.28), channel_id=1, source_target_pairs={{0,192},{32,224},{64,0},{96,32},{128,64},{160,96},{192,128},{224,1... | collective-permute-start | bytes 393224 | tf_op jit(solution)/shard_map/ppermute | solution.py:237
  101.2 17.8 %collective-permute-start.8 = (f32[128,256]{1,0:T(8,128)S(1)}, f32[128,256]{1,0:T(8,128)S(1)}, u32[]{:S(2)}, u32[]{:S(2)}) collective-permute-start(f32[128,256]{1,0:T(8,128)S(1)} %add.28), channel_id=1, source_target_pairs={{0,64},{32,96},{64,128},{96,160},{128,192},{160,224},{192,0},{224,... | collective-permute-start | bytes 393224 | tf_op jit(solution)/shard_map/ppermute | solution.py:237
  105.5 13.6 %collective-permute-start.7 = (f32[128,256]{1,0:T(8,128)S(1)}, f32[128,256]{1,0:T(8,128)S(1)}, u32[]{:S(2)}, u32[]{:S(2)}) collective-permute-start(f32[128,256]{1,0:T(8,128)S(1)} %add.28), channel_id=1, source_target_pairs={{0,160},{32,192},{64,224},{96,0},{128,32},{160,64},{192,96},{224,1... | collective-permute-start | bytes 393224 | tf_op jit(solution)/shard_map/ppermute | solution.py:237
  111.0 14.2 %collective-permute-start.6 = (f32[128,256]{1,0:T(8,128)S(1)}, f32[128,256]{1,0:T(8,128)S(1)}, u32[]{:S(2)}, u32[]{:S(2)}) collective-permute-start(f32[128,256]{1,0:T(8,128)S(1)} %add.28), channel_id=1, source_target_pairs={{0,96},{32,128},{64,160},{96,192},{128,224},{160,0},{192,32},{224,... | collective-permute-start | bytes 393224 | tf_op jit(solution)/shard_map/ppermute | solution.py:237
  113.8 17.9 %collective-permute-start.5 = (f32[128,256]{1,0:T(8,128)S(1)}, f32[128,256]{1,0:T(8,128)S(1)}, u32[]{:S(2)}, u32[]{:S(2)}) collective-permute-start(f32[128,256]{1,0:T(8,128)S(1)} %add.28), channel_id=1, source_target_pairs={{0,128},{32,160},{64,192},{96,224},{128,0},{160,32},{192,64},{224,... | collective-permute-start | bytes 393224 | tf_op jit(solution)/shard_map/ppermute | solution.py:237
  131.8 25.6 %collective-permute-start.12 = (f32[128,256]{1,0:T(8,128)S(1)}, f32[128,256]{1,0:T(8,128)S(1)}, u32[]{:S(2)}, u32[]{:S(2)}) collective-permute-start(f32[128,256]{1,0:T(8,128)S(1)} %add_add_fusion.kept_ref), channel_id=1, source_target_pairs={{0,256},{256,0},{1,257},{257,1},{2,258},{258,2},{3,259},{259,3},{4... | collective-permute-start | bytes 393224 | tf_op jit(solution)/shard_map/ppermute | solution.py:125

commit v3 on v2

--- a/solution.py
+++ b/solution.py
@@ -12,8 +12,8 @@
 NP = B // V
 X = 4
 Z = 8
-ROWS = 32
-SHARE_ROWS = B // Z
+PARTS = 4
+SHARE_ROWS = B // X
 HI = lax.Precision.HIGHEST
 F32 = jnp.float32
 
@@ -68,11 +68,11 @@
 
 
 def tile(g_ref, block, t):
-    s = block * SHARE_ROWS + (t % 2) * V
-    return g_ref[t // 2 * X + s // 40, s % 40 : s % 40 + V, :]
-
-
-def factor_kernel(g_ref, r_ref, w_ref, m_ref):
+    s = block * SHARE_ROWS + (t % 4) * V
+    return g_ref[s // 40 * X + t // 4, s % 40 : s % 40 + V, :]
+
+
+def factor_kernel(g_ref, after_ref, r_ref, w_ref, end_ref, m_ref):
     block = 0
     for i in range(NB):
         for j in range(i, NB):
@@ -98,21 +98,22 @@
                 if k:
                     m_ref[q : q + B, :o] = m_ref[q : q + B, :o] - mm(lt, w_ref[o:e, :o])
                 m_ref[q : q + B, o:e] = -mm(lt, v)
-
-
-def factor(shares):
+    end_ref[...] = jnp.zeros_like(end_ref)
+
+
+def factor(shares, after):
     out = jax.ShapeDtypeStruct((N, N), F32)
     vmem = pl.BlockSpec(memory_space=pltpu.VMEM)
     return pl.pallas_call(
         factor_kernel,
-        out_shape=(out, out),
+        out_shape=(out, out, jax.ShapeDtypeStruct((V, B), F32)),
         scratch_shapes=[pltpu.VMEM((N, N), F32)],
-        in_specs=[vmem],
-        out_specs=(vmem, vmem),
-        compiler_params=pltpu.CompilerParams(vmem_limit_bytes=32 * 2**20),
+        in_specs=[vmem, pl.BlockSpec(memory_space=pl.ANY)],
+        out_specs=(vmem, vmem, vmem),
+        compiler_params=pltpu.CompilerParams(vmem_limit_bytes=16 * 2**20),
         cost_estimate=pl.CostEstimate(flops=20_000_000_000, bytes_accessed=3 * 2**20, transcendentals=0),
         name="factor",
-    )(shares)
+    )(shares, after)
 
 
 def sent_to_all(x, axis, groups=None):
@@ -126,11 +127,11 @@
 
 
 VMEM = pl.BlockSpec(memory_space=pltpu.VMEM)
-PARAMS = pltpu.CompilerParams(vmem_limit_bytes=32 * 2**20)
+PARAMS = pltpu.CompilerParams(vmem_limit_bytes=16 * 2**20)
 
 
 def gram_kernel(p_ref, own_ref, t_ref):
-    first = lax.axis_index("dev") // X * SHARE_ROWS
+    first = lax.axis_index("dev") % X * SHARE_ROWS
     for i in range(NB):
         t_ref[i * B : (i + 1) * B, :] = p_ref[:, i * B : (i + 1) * B].T
     left = jnp.concatenate([t_ref[pl.ds(pl.multiple_of(i * B + first, SHARE_ROWS), SHARE_ROWS), :] for i in range(NB)], 0)
@@ -147,7 +148,7 @@
 def gram_shares(rows):
     return pl.pallas_call(
         gram_kernel,
-        out_shape=jax.ShapeDtypeStruct((X, 40, B), F32),
+        out_shape=jax.ShapeDtypeStruct((Z, 40, B), F32),
         scratch_shapes=[pltpu.VMEM((N, rows.shape[0]), F32)],
         in_specs=[VMEM],
         out_specs=VMEM,
@@ -156,16 +157,12 @@
     )(rows)
 
 
-def slab_rows(k, z):
-    x = (lax.axis_index("dev") + (X - k)) % X
-    return pl.ds(pl.multiple_of((z * X + x) * ROWS, ROWS), ROWS)
-
-
-def cross_kernel(p0, p1, p2, p3, t_ref, kept_ref, given_ref):
+def cross_kernel(p_ref, t_ref, kept_ref, given_ref):
+    rows = p_ref.shape[0] // PARTS
     total = None
-    for k, p_ref in enumerate((p0, p1, p2, p3)):
-        t = jnp.concatenate([t_ref[slab_rows(k, z), :] for z in range(Z)], 0)
-        part = mm(t.T, p_ref[...])
+    for i in range(PARTS):
+        here = slice(i * rows, (i + 1) * rows)
+        part = mm(t_ref[here, :].T, p_ref[here, :])
         total = part if total is None else total + part
     first = lax.axis_index("half") == 0
     low, high = total[:, : N // 2], total[:, N // 2 :]
@@ -173,73 +170,67 @@
     given_ref[...] = jnp.where(first, high, low)
 
 
-def cross_halves(blocks, trailing):
+def cross_halves(panel_group, trailing):
     out = jax.ShapeDtypeStruct((trailing.shape[1], N // 2), F32)
     return pl.pallas_call(
         cross_kernel,
         out_shape=(out, out),
-        in_specs=[VMEM] * 5,
+        in_specs=[VMEM] * 2,
         out_specs=(VMEM, VMEM),
         compiler_params=PARAMS,
         cost_estimate=pl.CostEstimate(flops=2_000_000_000, bytes_accessed=3 * 2**20, transcendentals=0),
         name="cross",
-    )(*blocks, trailing)
-
-
-def finish_kernel(w_ref, kept_ref, other_ref, p0, p1, p2, p3, t_ref, y_ref, r_ref):
+    )(panel_group, trailing)
+
+
+def finish_kernel(w_ref, kept_ref, other_ref, p_ref, t_ref, end_ref, y_ref, r_ref):
     first = lax.axis_index("half") == 0
     kept, other = kept_ref[...], other_ref[...]
     cross = jnp.concatenate([jnp.where(first, kept, other), jnp.where(first, other, kept)], 1)
     projected = mm(cross, w_ref[...], ((1,), (1,)))
     y_ref[...] = projected.T
     solved = mm(projected, w_ref[...])
-    for k, p_ref in enumerate((p0, p1, p2, p3)):
-        part = mm(p_ref[...], solved, ((1,), (1,)))
-        for z in range(Z):
-            here = slab_rows(k, z)
-            r_ref[here, :] = t_ref[here, :] - part[z * ROWS : (z + 1) * ROWS, :]
-
-
-def finish(inverse, kept, other, blocks, trailing):
+    r_ref[...] = t_ref[...] - mm(p_ref[...], solved, ((1,), (1,)))
+
+
+def finish(inverse, kept, other, panel_group, trailing, end):
     return pl.pallas_call(
         finish_kernel,
         out_shape=(
             jax.ShapeDtypeStruct((N, trailing.shape[1]), F32),
             jax.ShapeDtypeStruct(trailing.shape, F32),
         ),
-        in_specs=[VMEM] * 8,
+        in_specs=[VMEM] * 6,
         out_specs=(VMEM, VMEM),
         compiler_params=PARAMS,
         name="finish",
-    )(inverse, kept, other, *blocks, trailing)
+    )(inverse, kept, other, panel_group, trailing, end)
 
 
 def on_device(panel_block, trailing):
     along_x = [[z * X + x for x in range(X)] for z in range(Z)]
     along_z = [[z * X + x for z in range(Z)] for x in range(X)]
-    rows = sent_to_all(panel_block, "dev", along_z).reshape(-1, N)
+    groups = lax.axis_size("grp")
+    alternate = [list(range(first, groups, 2)) for first in range(2)]
+    rows = sent_to_all(panel_block, "dev", along_x).reshape(-1, N)
+    panel_group = lax.all_gather(rows, "dev", axis=0, axis_index_groups=along_z, tiled=True)
 
     own = gram_shares(rows)
-    share = lax.all_to_all(own, "dev", 0, 0, axis_index_groups=along_x, tiled=True).sum(0)
-    rows, _ = lax.optimization_barrier((rows, own))
-    blocks = [rows]
-    for k in range(1, X):
-        moves = [(z * X + x, z * X + (x + k) % X) for z in range(Z) for x in range(X)]
-        blocks.append(lax.ppermute(rows, "dev", moves))
+    share = lax.all_to_all(own, "dev", 0, 0, axis_index_groups=along_z, tiled=True).sum(0)
     share = share + swapped(share)
     share = sent_to_all(share, "grp").sum(0)
     shares = sent_to_all(share, "dev")
 
-    kept, given = cross_halves(blocks, trailing)
+    panel_group, _ = lax.optimization_barrier((panel_group, share))
+    kept, given = cross_halves(panel_group, trailing)
     kept = kept + swapped(given)
-    groups = lax.axis_size("grp")
-    kept, _ = lax.optimization_barrier((kept, share))
-    parts = [lax.ppermute(kept, "grp", [(g, (g + k) % groups) for g in range(groups)]) for k in (4, 3, 5, 2, 6, 1, 7)]
-    kept = sum(parts, kept)
+    kept = kept + lax.ppermute(kept, "grp", [(g, g ^ 1) for g in range(groups)])
+
+    triangle, inverse, end = factor(shares, kept)
+    kept = sent_to_all(kept, "grp", alternate).sum(0)
+    kept, end = lax.optimization_barrier((kept, end))
     other = swapped(kept)
-
-    triangle, inverse = factor(shares)
-    projected, remainder = finish(inverse, kept, other, blocks, trailing)
+    projected, remainder = finish(inverse, kept, other, panel_group, trailing, end)
     return (triangle, projected, remainder)
 
 

time: 162 us -> 133 us (0.82)
  the two profiles are of different devices: /device:TPU:17 before, /device:TPU:1 now
where the time goes in v3:
time: 133 us; the launch traced here: 132 us
  blocking collectives  43.9 us (33%)
  starting transfers between devices  29.7 us (22%)
  Pallas kernels  28.1 us (21%)
  between operations  14.2 us (11%)
  waiting for transfers between devices  8.02 us (6%)
  local copies, waits for them, and re-layouts  7.43 us (6%)
    all_to_all x2, blocking collectives, sent_to_all(): lax.all_to_all(copies, axis, 0, 0, axis_index_groups=groups, tiled=True)  25.7 us
    pallas_call x1, Pallas kernels, factor(): pl.pallas_call(factor_kernel, out_shape=(out, out, jax.ShapeDtypeStruct((...  22.1 us
    all_to_all x1, blocking collectives, on_device(): lax.all_to_all(own, 'dev', 0, 0, axis_index_groups=along_z, tiled=True)  18.3 us
    ppermute x3, starting transfers between devices, swapped(): return lax.ppermute(x, 'half', [(0, 1), (1, 0)])  14.3 us
    all_to_all x2, starting transfers between devices, sent_to_all(): lax.all_to_all(copies, axis, 0, 0, axis_index_groups=groups, tiled=True)  12.2 us
    unnamed x14, local copies, waits for them, and re-layouts  4.79 us
    pallas_call x1, Pallas kernels, finish(): pl.pallas_call(finish_kernel, out_shape=(jax.ShapeDtypeStruct((N, trailin...  4.37 us
    ppermute x1, waiting for transfers between devices, on_device(): kept = kept + lax.ppermute(kept, 'grp', [(g, g ^ 1) for g in range(groups)])  3.49 us
  transfers between devices with their start and end apart: 7, of which 5 were waited for; matrix products, arithmetic and copies ran while one was open for 1% of the time, Pallas kernels for 18%

profile of v3, /device:TPU:1, one launch (start us, length us, event | category | flops | bytes accessed | tf_op | source)
XLA Modules:
  0.0 132.5 jit_solution(11677069486845345391)
XLA Ops:
  7.2 0.0 all-gather.2.cloned.1.call-start
  7.2 0.9 broadcast_in_dim.8
  8.1 0.0 copy-start.5
  8.1 10.4 %all_to_all.25 = f32[4,32,512]{2,1,0:T(8,128)} all-to-all(f32[4,32,512]{2,1,0:T(8,128)S(1)} %broadcast_in_dim.8), channel_id=1, replica_groups={{0,1,2,3},{4,5,6,7},{8,9,10,11},{12,13,14,15},{16,17,18,19},{20,21,22,2..., dimensions={0} | all-to-all | bytes 524288 | tf_op jit(solution)/shard_map/all_to_all | solution.py:122
  18.5 0.0 all-gather.2.cloned.1.call-update
  18.5 0.0 copy-start
  18.5 0.9 copy-done
  19.5 0.5 gram.1
  20.0 18.3 %all_to_all.26 = f32[8,40,128]{2,1,0:T(8,128)S(1)} all-to-all(f32[8,40,128]{2,1,0:T(8,128)S(1)} %gram.1), channel_id=1, replica_groups={{0,4,8,12,16,20,24,28},{1,5,9,13,17,21,25,29},{2,6,10,14,18,22,26,30},{..., dimensions={0} | all-to-all | bytes 327680 | tf_op jit(solution)/shard_map/all_to_all | solution.py:219
  38.2 5.3 %collective-permute-start = (f32[40,128]{1,0:T(8,128)S(1)}, f32[40,128]{1,0:T(8,128)S(1)}, u32[]{:S(2)}, u32[]{:S(2)}) collective-permute-start(f32[40,128]{1,0:T(8,128)S(1)} %reduce_sum.27), channel_id=1, source_target_pairs={{0,256},{256,0},{1,257},{257,1},{2,258},{258,2},{3,259},{259,3},{4... | collective-permute-start | bytes 61448 | tf_op jit(solution)/shard_map/ppermute | solution.py:126
  43.5 0.8 collective-permute-done
  44.4 15.3 %all_to_all.27 = f32[8,40,128]{2,1,0:T(8,128)S(1)} all-to-all(f32[8,40,128]{2,1,0:T(8,128)S(1)} %broadcast_in_dim.9), channel_id=1, replica_groups=mesh['half'=2,'grp'=8,'dev'=32] {'grp'}, dimensions={0} | all-to-all | bytes 327680 | tf_op jit(solution)/shard_map/all_to_all | solution.py:122
  59.7 0.9 broadcast_in_dim.10
  60.6 3.9 %all-to-all-start.3 = ((f32[32,40,128]{2,1,0:T(8,128)}), f32[32,40,128]{2,1,0:T(8,128)S(1)}, u32[]{:S(2)}, u32[]{:S(2)}) async-start(f32[32,40,128]{2,1,0:T(8,128)} %broadcast_in_dim.10), calls=%async_computation.3 | async-start | bytes 1310720 | tf_op jit(solution)/shard_map/all_to_all | solution.py:122
  64.5 0.0 all-gather.2.cloned.1.call-done.p_ref
  64.5 0.0 copy-done.5
  64.5 0.0 copy-start.1
  64.5 1.6 %copy-done.1 = f32[1024,512]{1,0:T(8,128)S(1)} copy-done((f32[1024,512]{1,0:T(8,128)S(1)}, f32[1024,512]{1,0:T(8,128)}, u32[]{:S(2)}) %copy-start.1) | copy-done | bytes 2097176
  66.1 1.1 cross.1
  67.2 5.6 %collective-permute-start.1 = (f32[128,256]{1,0:T(8,128)S(1)}, f32[128,256]{1,0:T(8,128)S(1)}, u32[]{:S(2)}, u32[]{:S(2)}) collective-permute-start(f32[128,256]{1,0:T(8,128)S(1)} %get-tuple-element.15), channel_id=1, source_target_pairs={{0,256},{256,0},{1,257},{257,1},{2,258},{258,2},{3,259},{259,3},{4... | collective-permute-start | bytes 393224 | tf_op jit(solution)/shard_map/ppermute | solution.py:126
  72.9 1.0 collective-permute-done.1
  73.9 3.1 %collective-permute-start.2 = (f32[128,256]{1,0:T(8,128)S(1)}, f32[128,256]{1,0:T(8,128)S(1)}, u32[]{:S(2)}, u32[]{:S(2)}) collective-permute-start(f32[128,256]{1,0:T(8,128)S(1)} %add.10), channel_id=1, source_target_pairs={{0,32},{32,0},{64,96},{96,64},{128,160},{160,128},{192,224},{224,1... | collective-permute-start | bytes 393224 | tf_op jit(solution)/shard_map/ppermute | solution.py:227
  77.0 3.5 %collective-permute-done.2 = f32[128,256]{1,0:T(8,128)S(1)} collective-permute-done((f32[128,256]{1,0:T(8,128)S(1)}, f32[128,256]{1,0:T(8,128)S(1)}, u32[]{:S(2)}, u32[]{:S(2)}) %collective-permute-start.2) | collective-permute-done | bytes 131104 | tf_op jit(solution)/shard_map/ppermute | solution.py:227
  80.5 1.7 %all-to-all-done.3.g_ref = f32[32,40,128]{2,1,0:T(8,128)S(1)} async-done(((f32[32,40,128]{2,1,0:T(8,128)}), f32[32,40,128]{2,1,0:T(8,128)S(1)}, u32[]{:S(2)}, u32[]{:S(2)}) %all-to-all-start.3) | async-done | bytes 655392 | tf_op jit(solution)/shard_map/all_to_all | solution.py:122
  82.3 0.0 copy-start.3
  82.3 0.9 broadcast_in_dim.11
  83.1 0.1 copy-done.3
  83.3 8.3 %all-to-all-start.4 = ((f32[4,128,256]{2,1,0:T(8,128)}), f32[4,128,256]{2,1,0:T(8,128)}, u32[]{:S(2)}, u32[]{:S(2)}) async-start(f32[4,128,256]{2,1,0:T(8,128)} %broadcast_in_dim.11), calls=%async_computation.4 | async-start | bytes 1048576 | tf_op jit(solution)/shard_map/all_to_all | solution.py:122
  91.6 0.0 copy-start.4
  91.6 1.1 copy-done.4
  92.7 0.0 copy-start.2
  92.7 22.1 %factor.1 = (f32[512,512]{1,0:T(8,128)}, f32[512,512]{1,0:T(8,128)S(1)}, f32[8,128]{1,0:T(8,128)S(1)}) custom-call(f32[32,40,128]{2,1,0:T(8,128)S(1)} %copy-done.4, f32[128,256]{1,0:T(8,128)S(1)} %add.11.after_ref), custom_call_target="tpu_custom_call" | custom-call | flops 20000000000 | bytes 3145728 | tf_op jit(solution)/shard_map/factor/pallas_call | solution.py:107
  114.8 0.0 all-to-all-done.4
  114.8 1.1 reduce_sum.29.kept_ref
  115.9 3.4 %collective-permute-start.3 = (f32[128,256]{1,0:T(8,128)S(1)}, f32[128,256]{1,0:T(8,128)S(1)}, u32[]{:S(2)}, u32[]{:S(2)}) collective-permute-start(f32[128,256]{1,0:T(8,128)S(1)} %reduce_sum.29.kept_ref), channel_id=1, source_target_pairs={{0,256},{256,0},{1,257},{257,1},{2,258},{258,2},{3,259},{259,3},{4... | collective-permute-start | bytes 393224 | tf_op jit(solution)/shard_map/ppermute | solution.py:126
  119.2 1.0 collective-permute-done.3.other_ref
  120.2 0.0 copy-done.2
  120.2 0.0 copy-start.6
  120.2 1.0 copy-done.6
  121.2 4.4 %finish.1 = (f32[512,128]{1,0:T(8,128)}, f32[1024,128]{1,0:T(8,128)}) custom-call(f32[512,512]{1,0:T(8,128)S(1)} %get-tuple-element.17.w_ref, f32[128,256]{1,0:T(8,128)S(1)} %reduce_sum.29.kept_ref, f32[128,256]{1,0:T(8,128)S(1)} %collective-permute-done.3.other_ref, f32[1024,512]{1,0:T(8,128)S(1)} %copy-done.2, f32[1024,128]{1,0:T(8,128)S(1)} %copy-done.6, ...), custom_call_target="tpu_custom_call" | custom-call | tf_op jit(solution)/shard_map/finish/pallas_call | solution.py:197
  (6 shorter events, 0.1 us)
Async XLA Ops:
  7.2 57.3 %all-gather.2.cloned.1.call-start = ((), (), s32[]{:S(2)}) async-start(), calls=%async_computation.5 | async-start | bytes 2359296 | tf_op jit(solution)/shard_map/all_gather | solution.py:216
  8.1 56.4 %copy-start.5 = (f32[1024,128]{1,0:T(8,128)S(1)}, f32[1024,128]{1,0:T(8,128)}, u32[]{:S(2)}) copy-start(f32[1024,128]{1,0:T(8,128)} %t_ref.3) | copy-start | bytes 1572868
  18.5 1.0 copy-start
  38.2 6.1 %collective-permute-start = (f32[40,128]{1,0:T(8,128)S(1)}, f32[40,128]{1,0:T(8,128)S(1)}, u32[]{:S(2)}, u32[]{:S(2)}) collective-permute-start(f32[40,128]{1,0:T(8,128)S(1)} %reduce_sum.27), channel_id=1, source_target_pairs={{0,256},{256,0},{1,257},{257,1},{2,258},{258,2},{3,259},{259,3},{4... | collective-permute-start | bytes 61448 | tf_op jit(solution)/shard_map/ppermute | solution.py:126
  60.6 21.7 %all-to-all-start.3 = ((f32[32,40,128]{2,1,0:T(8,128)}), f32[32,40,128]{2,1,0:T(8,128)S(1)}, u32[]{:S(2)}, u32[]{:S(2)}) async-start(f32[32,40,128]{2,1,0:T(8,128)} %broadcast_in_dim.10), calls=%async_computation.3 | async-start | bytes 1310720 | tf_op jit(solution)/shard_map/all_to_all | solution.py:122
  64.5 1.6 %copy-start.1 = (f32[1024,512]{1,0:T(8,128)S(1)}, f32[1024,512]{1,0:T(8,128)}, u32[]{:S(2)}) copy-start(f32[1024,512]{1,0:T(8,128)} %all-gather.2.cloned.1.call-done.p_ref) | copy-start | bytes 6291460
  67.2 6.6 %collective-permute-start.1 = (f32[128,256]{1,0:T(8,128)S(1)}, f32[128,256]{1,0:T(8,128)S(1)}, u32[]{:S(2)}, u32[]{:S(2)}) collective-permute-start(f32[128,256]{1,0:T(8,128)S(1)} %get-tuple-element.15), channel_id=1, source_target_pairs={{0,256},{256,0},{1,257},{257,1},{2,258},{258,2},{3,259},{259,3},{4... | collective-permute-start | bytes 393224 | tf_op jit(solution)/shard_map/ppermute | solution.py:126
  73.9 6.6 %collective-permute-start.2 = (f32[128,256]{1,0:T(8,128)S(1)}, f32[128,256]{1,0:T(8,128)S(1)}, u32[]{:S(2)}, u32[]{:S(2)}) collective-permute-start(f32[128,256]{1,0:T(8,128)S(1)} %add.10), channel_id=1, source_target_pairs={{0,32},{32,0},{64,96},{96,64},{128,160},{160,128},{192,224},{224,1... | collective-permute-start | bytes 393224 | tf_op jit(solution)/shard_map/ppermute | solution.py:227
  82.3 1.0 copy-start.3
  83.3 31.5 %all-to-all-start.4 = ((f32[4,128,256]{2,1,0:T(8,128)}), f32[4,128,256]{2,1,0:T(8,128)}, u32[]{:S(2)}, u32[]{:S(2)}) async-start(f32[4,128,256]{2,1,0:T(8,128)} %broadcast_in_dim.11), calls=%async_computation.4 | async-start | bytes 1048576 | tf_op jit(solution)/shard_map/all_to_all | solution.py:122
  91.6 1.1 copy-start.4
  92.7 27.5 %copy-start.2 = (f32[1024,512]{1,0:T(8,128)S(1)}, f32[1024,512]{1,0:T(8,128)}, u32[]{:S(2)}) copy-start(f32[1024,512]{1,0:T(8,128)} %all-gather.2.cloned.1.call-done.p_ref) | copy-start | bytes 6291460
  115.9 4.3 %collective-permute-start.3 = (f32[128,256]{1,0:T(8,128)S(1)}, f32[128,256]{1,0:T(8,128)S(1)}, u32[]{:S(2)}, u32[]{:S(2)}) collective-permute-start(f32[128,256]{1,0:T(8,128)S(1)} %reduce_sum.29.kept_ref), channel_id=1, source_target_pairs={{0,256},{256,0},{1,257},{257,1},{2,258},{258,2},{3,259},{259,3},{4... | collective-permute-start | bytes 393224 | tf_op jit(solution)/shard_map/ppermute | solution.py:126
  120.2 1.0 copy-start.6
Sparse Core Ops, SparseCore 0:
  18.6 44.8 all-gather.1

commit v4 on v3

--- a/solution.py
+++ b/solution.py
@@ -13,9 +13,38 @@
 X = 4
 Z = 8
 PARTS = 4
+GROUP = 4
 SHARE_ROWS = B // X
 HI = lax.Precision.HIGHEST
 F32 = jnp.float32
+BF16 = jnp.bfloat16
+VMEM = pl.BlockSpec(memory_space=pltpu.VMEM)
+PARAMS = pltpu.CompilerParams(vmem_limit_bytes=16 * 2**20)
+
+
+def mm(a, b, dims=((1,), (0,))):
+    return lax.dot_general(a, b, (dims, ((), ())), precision=HI, preferred_element_type=F32)
+
+
+def three(x):
+    high = x.astype(BF16)
+    rest = x - high.astype(F32)
+    middle = rest.astype(BF16)
+    return high, middle, (rest - middle.astype(F32)).astype(BF16)
+
+
+def left(x, axis):
+    h, m, l = three(x)
+    return jnp.concatenate([h, h, m, m, h, l], axis)
+
+
+def right(x, axis):
+    h, m, l = three(x)
+    return jnp.concatenate([h, m, h, m, l, h], axis)
+
+
+def dot(a, b, dims):
+    return lax.dot_general(a, b, (dims, ((), ())), preferred_element_type=F32)
 
 
 def across_lanes(v, c):
@@ -24,51 +53,78 @@
 
 def across_rows(v, j):
     return jnp.broadcast_to(v[j : j + 1, :], (V, B))
+
+
+def eliminated(x, m0, m1, j, keep):
+    return jnp.where(keep, x, 0.0) - m0 * across_rows(x, j) - m1 * across_rows(x, j + 1)
+
+
+def total(terms):
+    while len(terms) > 1:
+        terms = [terms[i] + terms[i + 1] for i in range(0, len(terms), 2)]
+    return terms[0]
 
 
 def factor_block(m):
     row = lax.broadcasted_iota(jnp.int32, (V, B), 0)
     lane = lax.broadcasted_iota(jnp.int32, (V, B), 1)
-    ups, invs = [], []
+    ups, invs, b = [], [], None
     for p in range(NP):
         r0 = p * V
         mp = m[p]
         diag = (lane >= r0) & (lane < r0 + V)
         eye = (lane == row + r0).astype(F32)
-        b = [across_lanes(mp, r0 + j) for j in range(V)]
+        more = p + 1 < NP
+        if b is None:
+            b = [across_lanes(mp, r0 + j) for j in range(V)]
+        ahead = [across_lanes(mp, r0 + V + j) for j in range(V)] if more else []
         low, low_e, full = mp, eye, jnp.where(diag, eye, mp)
         dv = jnp.ones((V, B), F32)
-        for j in range(V):
-            d = across_rows(b[j], j)
-            dv = jnp.where(row == j, d, dv)
-            mult = b[j] * (1.0 / d)
-            mfull = jnp.where(row == j, 0.0, mult)
-            mlow = jnp.where(row > j, mult, 0.0)
-            for k in range(j + 1, V):
-                b[k] = b[k] - mfull * across_rows(b[k], j)
-            low = low - mlow * across_rows(low, j)
-            low_e = low_e - mlow * across_rows(low_e, j)
-            full = full - mfull * across_rows(full, j)
+        for j in range(0, V, 2):
+            d, x, c = across_rows(b[j], j), across_rows(b[j], j + 1), across_rows(b[j + 1], j + 1)
+            det = d * c - x * x
+            over_det, over_d = 1.0 / det, 1.0 / d
+            u0, u1 = b[j] * c - b[j + 1] * x, b[j + 1] * d - b[j] * x
+            first, second, below = row == j, row == j + 1, row > j + 1
+            keep = ~(first | second)
+            m0 = jnp.where(first, -c, jnp.where(second, x, u0)) * over_det
+            m1 = jnp.where(first, x, jnp.where(second, -d, u1)) * over_det
+            for k in range(j + 2, V):
+                b[k] = eliminated(b[k], m0, m1, j, keep)
+            ahead = [eliminated(n, m0, m1, j, keep) for n in ahead]
+            l0 = jnp.where(below, m0, jnp.where(second, x * over_d, 0.0))
+            l1 = jnp.where(below, m1, 0.0)
+            low = low - l0 * across_rows(low, j) - l1 * across_rows(low, j + 1)
+            low_e = low_e - l0 * across_rows(low_e, j) - l1 * across_rows(low_e, j + 1)
+            full = eliminated(full, m0, m1, j, keep)
+            dv = jnp.where(first, d, jnp.where(second, det * over_d, dv))
         rs = lax.rsqrt(dv)
-        full = full * (1.0 / dv)
         ups.append(jnp.where(lane >= row + r0, low * rs, 0.0))
         invs.append(jnp.where(lane <= row + r0, jnp.where(diag, low_e, low) * rs, 0.0))
-        if p + 1 < NP:
-            f = [across_rows(full, j) for j in range(V)]
-            for q in range(p + 1, NP):
-                old = m[q]
-                t = [across_lanes(old, r0 + j) * f[j] for j in range(V)]
-                s = ((t[0] + t[1]) + (t[2] + t[3])) + ((t[4] + t[5]) + (t[6] + t[7]))
-                m[q] = jnp.where(diag, 0.0, old) - s
+        if not more:
+            break
+        end = (p // GROUP + 1) * GROUP
+        here = [across_lanes(m[p + 1], r0 + j) for j in range(V)]
+        b = [
+            across_lanes(m[p + 1], r0 + V + k) - total([here[j] * across_rows(ahead[k], j) for j in range(V)])
+            for k in range(V)
+        ]
+        f = [across_rows(full, j) for j in range(V)]
+        for q in range(p + 1, min(end + 1, NP)):
+            old = m[q]
+            m[q] = jnp.where(diag, 0.0, old) - total([across_lanes(old, r0 + j) * f[j] for j in range(V)])
+        if p + 1 == end and end + 1 < NP:
+            u, w = jnp.concatenate(ups[-GROUP:], 0), jnp.concatenate(invs[-GROUP:], 0)
+            inverse_lanes = lax.broadcasted_iota(jnp.int32, u.shape, 1) < end * V
+            update = dot(left(u, 0), right(jnp.where(inverse_lanes, w, u), 0), ((0,), (0,)))
+            done = (lane >= (end - GROUP) * V) & (lane < end * V)
+            for q in range(end + 1, NP):
+                m[q] = jnp.where(done, 0.0, m[q]) - update[q * V : (q + 1) * V, :]
     return jnp.concatenate(ups, 0), jnp.concatenate(invs, 0)
 
 
-def mm(a, b, dims=((1,), (0,))):
-    return lax.dot_general(a, b, (dims, ((), ())), precision=HI, preferred_element_type=F32)
-
-
 def tile(g_ref, block, t):
-    s = block * SHARE_ROWS + (t % 4) * V
+    s = block * SHARE_ROWS + t % 4 * V
     return g_ref[s // 40 * X + t // 4, s % 40 : s % 40 + V, :]
 
 
@@ -79,38 +135,42 @@
             for t in range(NP):
                 m_ref[i * B + V * t : i * B + V * (t + 1), j * B : (j + 1) * B] = tile(g_ref, block, t)
             block += 1
-    r_ref[...] = jnp.zeros_like(r_ref)
     for k in range(NB):
         o = k * B
         e = o + B
+        f = e + B
         u, v = factor_block([m_ref[o + V * i : o + V * (i + 1), o:e] for i in range(NP)])
+        v_left = left(v, 1)
         r_ref[o:e, o:e] = u
         w_ref[o:e, o:e] = v
+        if e < N:
+            ps = dot(v_left, right(m_ref[o:e, e:], 0), ((1,), (0,)))
+            r_ref[o:e, e:] = ps
+            w_ref[o:e, e:] = jnp.zeros((B, N - e), F32)
+            p_left, p_right = left(ps, 0), right(ps, 0)
+            m_ref[e:f, e:] = m_ref[e:f, e:] - dot(p_left[:, :B], p_right, ((0,), (0,)))
+            if f < N:
+                m_ref[f:, f:] = m_ref[f:, f:] - dot(p_left[:, B:], p_right[:, B:], ((0,), (0,)))
         if k:
-            w_ref[o:e, :o] = mm(v, m_ref[o:e, :o])
-        if k + 1 < NB:
-            w_ref[o:e, e:] = jnp.zeros((B, N - e), F32)
-            ps = mm(v, m_ref[o:e, e:])
-            r_ref[o:e, e:] = ps
-            for i in range(k + 1, NB):
-                q, lt = i * B, ps[:, (i - k - 1) * B : (i - k) * B].T
-                m_ref[q : q + B, q:] = m_ref[q : q + B, q:] - mm(lt, ps[:, q - e :])
-                if k:
-                    m_ref[q : q + B, :o] = m_ref[q : q + B, :o] - mm(lt, w_ref[o:e, :o])
-                m_ref[q : q + B, o:e] = -mm(lt, v)
+            wl = dot(v_left, right(m_ref[o:e, :o], 0), ((1,), (0,)))
+            w_ref[o:e, :o] = wl
+            r_ref[o:e, :o] = jnp.zeros((B, o), F32)
+        if e < N:
+            if k:
+                m_ref[e:, :o] = m_ref[e:, :o] - dot(p_left, right(wl, 0), ((0,), (0,)))
+            m_ref[e:, o:e] = -dot(p_left, right(v, 0), ((0,), (0,)))
     end_ref[...] = jnp.zeros_like(end_ref)
 
 
 def factor(shares, after):
     out = jax.ShapeDtypeStruct((N, N), F32)
-    vmem = pl.BlockSpec(memory_space=pltpu.VMEM)
     return pl.pallas_call(
         factor_kernel,
         out_shape=(out, out, jax.ShapeDtypeStruct((V, B), F32)),
         scratch_shapes=[pltpu.VMEM((N, N), F32)],
-        in_specs=[vmem, pl.BlockSpec(memory_space=pl.ANY)],
-        out_specs=(vmem, vmem, vmem),
-        compiler_params=pltpu.CompilerParams(vmem_limit_bytes=16 * 2**20),
+        in_specs=[VMEM, pl.BlockSpec(memory_space=pl.ANY)],
+        out_specs=(VMEM, VMEM, VMEM),
+        compiler_params=PARAMS,
         cost_estimate=pl.CostEstimate(flops=20_000_000_000, bytes_accessed=3 * 2**20, transcendentals=0),
         name="factor",
     )(shares, after)
@@ -124,10 +184,6 @@
 
 def swapped(x):
     return lax.ppermute(x, "half", [(0, 1), (1, 0)])
-
-
-VMEM = pl.BlockSpec(memory_space=pltpu.VMEM)
-PARAMS = pltpu.CompilerParams(vmem_limit_bytes=16 * 2**20)
 
 
 def gram_kernel(p_ref, own_ref, t_ref):
@@ -159,13 +215,13 @@
 
 def cross_kernel(p_ref, t_ref, kept_ref, given_ref):
     rows = p_ref.shape[0] // PARTS
-    total = None
+    product = None
     for i in range(PARTS):
         here = slice(i * rows, (i + 1) * rows)
         part = mm(t_ref[here, :].T, p_ref[here, :])
-        total = part if total is None else total + part
+        product = part if product is None else product + part
     first = lax.axis_index("half") == 0
-    low, high = total[:, : N // 2], total[:, N // 2 :]
+    low, high = product[:, : N // 2], product[:, N // 2 :]
     kept_ref[...] = jnp.where(first, low, high)
     given_ref[...] = jnp.where(first, high, low)
 
@@ -176,7 +232,7 @@
         cross_kernel,
         out_shape=(out, out),
         in_specs=[VMEM] * 2,
-        out_specs=(VMEM, VMEM),
+        out_specs=(VMEM,) * 2,
         compiler_params=PARAMS,
         cost_estimate=pl.CostEstimate(flops=2_000_000_000, bytes_accessed=3 * 2**20, transcendentals=0),
         name="cross",

time: 133 us -> 125 us (0.940)
  Pallas kernels: 28.1 us -> 20.1 us
    pallas_call x1, Pallas kernels: 22.1 us -> 14.1 us  [factor(): pl.pallas_call(factor_kernel, out_shape=(out, out, jax.ShapeDtypeStruct((...]
  transfers between devices with their start and end apart: 7 -> 7, of which waited for: 5 -> 5; matrix products, arithmetic and copies ran while one was open for 1% -> 1% of each run, Pallas kernels for 18% -> 13%
where the time goes in v4:
time: 125 us
  blocking collectives  43.9 us (35%)
  starting transfers between devices  29.9 us (24%)
  Pallas kernels  20.1 us (16%)
  between operations  14.2 us (11%)
  waiting for transfers between devices  7.8 us (6%)
  local copies, waits for them, and re-layouts  7.43 us (6%)
    all_to_all x2, blocking collectives, sent_to_all(): lax.all_to_all(copies, axis, 0, 0, axis_index_groups=groups, tiled=True)  25.7 us
    all_to_all x1, blocking collectives, on_device(): lax.all_to_all(own, 'dev', 0, 0, axis_index_groups=along_z, tiled=True)  18.3 us
    ppermute x3, starting transfers between devices, swapped(): return lax.ppermute(x, 'half', [(0, 1), (1, 0)])  14.5 us
    pallas_call x1, Pallas kernels, factor(): pl.pallas_call(factor_kernel, out_shape=(out, out, jax.ShapeDtypeStruct((...  14.1 us
    all_to_all x2, starting transfers between devices, sent_to_all(): lax.all_to_all(copies, axis, 0, 0, axis_index_groups=groups, tiled=True)  12.2 us
    unnamed x14, local copies, waits for them, and re-layouts  4.78 us
    pallas_call x1, Pallas kernels, finish(): pl.pallas_call(finish_kernel, out_shape=(jax.ShapeDtypeStruct((N, trailin...  4.37 us
    ppermute x1, waiting for transfers between devices, on_device(): kept = kept + lax.ppermute(kept, 'grp', [(g, g ^ 1) for g in range(groups)])  3.49 us
  transfers between devices with their start and end apart: 7, of which 5 were waited for; matrix products, arithmetic and copies ran while one was open for 1% of the time, Pallas kernels for 13%

profile of v4, /device:TPU:1, one launch (start us, length us, event | category | flops | bytes accessed | tf_op | source)
XLA Modules:
  0.0 124.5 jit_solution(6852154824612214939)
XLA Ops:
  7.2 0.0 all-gather.2.cloned.1.call-start
  7.2 0.9 broadcast_in_dim.8
  8.1 0.0 copy-start.5
  8.1 10.4 %all_to_all.25 = f32[4,32,512]{2,1,0:T(8,128)} all-to-all(f32[4,32,512]{2,1,0:T(8,128)S(1)} %broadcast_in_dim.8), channel_id=1, replica_groups={{0,1,2,3},{4,5,6,7},{8,9,10,11},{12,13,14,15},{16,17,18,19},{20,21,22,2..., dimensions={0} | all-to-all | bytes 524288 | tf_op jit(solution)/shard_map/all_to_all | solution.py:182
  18.5 0.0 all-gather.2.cloned.1.call-update
  18.5 0.0 copy-start
  18.5 0.9 copy-done
  19.5 0.5 gram.1
  20.0 18.3 %all_to_all.26 = f32[8,40,128]{2,1,0:T(8,128)S(1)} all-to-all(f32[8,40,128]{2,1,0:T(8,128)S(1)} %gram.1), channel_id=1, replica_groups={{0,4,8,12,16,20,24,28},{1,5,9,13,17,21,25,29},{2,6,10,14,18,22,26,30},{..., dimensions={0} | all-to-all | bytes 327680 | tf_op jit(solution)/shard_map/all_to_all | solution.py:275
  38.2 5.3 %collective-permute-start = (f32[40,128]{1,0:T(8,128)S(1)}, f32[40,128]{1,0:T(8,128)S(1)}, u32[]{:S(2)}, u32[]{:S(2)}) collective-permute-start(f32[40,128]{1,0:T(8,128)S(1)} %reduce_sum.27), channel_id=1, source_target_pairs={{0,256},{256,0},{1,257},{257,1},{2,258},{258,2},{3,259},{259,3},{4... | collective-permute-start | bytes 61448 | tf_op jit(solution)/shard_map/ppermute | solution.py:186
  43.5 0.8 collective-permute-done
  44.4 15.3 %all_to_all.27 = f32[8,40,128]{2,1,0:T(8,128)S(1)} all-to-all(f32[8,40,128]{2,1,0:T(8,128)S(1)} %broadcast_in_dim.9), channel_id=1, replica_groups=mesh['half'=2,'grp'=8,'dev'=32] {'grp'}, dimensions={0} | all-to-all | bytes 327680 | tf_op jit(solution)/shard_map/all_to_all | solution.py:182
  59.7 0.9 broadcast_in_dim.10
  60.6 3.9 %all-to-all-start.3 = ((f32[32,40,128]{2,1,0:T(8,128)}), f32[32,40,128]{2,1,0:T(8,128)S(1)}, u32[]{:S(2)}, u32[]{:S(2)}) async-start(f32[32,40,128]{2,1,0:T(8,128)} %broadcast_in_dim.10), calls=%async_computation.3 | async-start | bytes 1310720 | tf_op jit(solution)/shard_map/all_to_all | solution.py:182
  64.5 0.0 all-gather.2.cloned.1.call-done.p_ref
  64.5 0.0 copy-done.5
  64.5 0.0 copy-start.1
  64.5 1.6 %copy-done.1 = f32[1024,512]{1,0:T(8,128)S(1)} copy-done((f32[1024,512]{1,0:T(8,128)S(1)}, f32[1024,512]{1,0:T(8,128)}, u32[]{:S(2)}) %copy-start.1) | copy-done | bytes 2097176
  66.1 1.1 cross.1
  67.2 5.6 %collective-permute-start.1 = (f32[128,256]{1,0:T(8,128)S(1)}, f32[128,256]{1,0:T(8,128)S(1)}, u32[]{:S(2)}, u32[]{:S(2)}) collective-permute-start(f32[128,256]{1,0:T(8,128)S(1)} %get-tuple-element.15), channel_id=1, source_target_pairs={{0,256},{256,0},{1,257},{257,1},{2,258},{258,2},{3,259},{259,3},{4... | collective-permute-start | bytes 393224 | tf_op jit(solution)/shard_map/ppermute | solution.py:186
  72.9 1.0 collective-permute-done.1
  73.9 3.1 %collective-permute-start.2 = (f32[128,256]{1,0:T(8,128)S(1)}, f32[128,256]{1,0:T(8,128)S(1)}, u32[]{:S(2)}, u32[]{:S(2)}) collective-permute-start(f32[128,256]{1,0:T(8,128)S(1)} %add.10), channel_id=1, source_target_pairs={{0,32},{32,0},{64,96},{96,64},{128,160},{160,128},{192,224},{224,1... | collective-permute-start | bytes 393224 | tf_op jit(solution)/shard_map/ppermute | solution.py:283
  77.0 3.5 %collective-permute-done.2 = f32[128,256]{1,0:T(8,128)S(1)} collective-permute-done((f32[128,256]{1,0:T(8,128)S(1)}, f32[128,256]{1,0:T(8,128)S(1)}, u32[]{:S(2)}, u32[]{:S(2)}) %collective-permute-start.2) | collective-permute-done | bytes 131104 | tf_op jit(solution)/shard_map/ppermute | solution.py:283
  80.5 1.7 %all-to-all-done.3.g_ref = f32[32,40,128]{2,1,0:T(8,128)S(1)} async-done(((f32[32,40,128]{2,1,0:T(8,128)}), f32[32,40,128]{2,1,0:T(8,128)S(1)}, u32[]{:S(2)}, u32[]{:S(2)}) %all-to-all-start.3) | async-done | bytes 655392 | tf_op jit(solution)/shard_map/all_to_all | solution.py:182
  82.3 0.0 copy-start.3
  82.3 0.9 broadcast_in_dim.11
  83.1 0.1 copy-done.3
  83.3 8.3 %all-to-all-start.4 = ((f32[4,128,256]{2,1,0:T(8,128)}), f32[4,128,256]{2,1,0:T(8,128)}, u32[]{:S(2)}, u32[]{:S(2)}) async-start(f32[4,128,256]{2,1,0:T(8,128)} %broadcast_in_dim.11), calls=%async_computation.4 | async-start | bytes 1048576 | tf_op jit(solution)/shard_map/all_to_all | solution.py:182
  91.6 0.0 copy-start.4
  91.6 1.1 copy-done.4
  92.7 0.0 copy-start.2
  92.7 14.1 %factor.1 = (f32[512,512]{1,0:T(8,128)}, f32[512,512]{1,0:T(8,128)S(1)}, f32[8,128]{1,0:T(8,128)S(1)}) custom-call(f32[32,40,128]{2,1,0:T(8,128)S(1)} %copy-done.4, f32[128,256]{1,0:T(8,128)S(1)} %add.11.after_ref), custom_call_target="tpu_custom_call" | custom-call | flops 20000000000 | bytes 3145728 | tf_op jit(solution)/shard_map/factor/pallas_call | solution.py:167
  106.8 0.0 all-to-all-done.4
  106.8 1.1 reduce_sum.29.kept_ref
  107.9 3.6 %collective-permute-start.3 = (f32[128,256]{1,0:T(8,128)S(1)}, f32[128,256]{1,0:T(8,128)S(1)}, u32[]{:S(2)}, u32[]{:S(2)}) collective-permute-start(f32[128,256]{1,0:T(8,128)S(1)} %reduce_sum.29.kept_ref), channel_id=1, source_target_pairs={{0,256},{256,0},{1,257},{257,1},{2,258},{258,2},{3,259},{259,3},{4... | collective-permute-start | bytes 393224 | tf_op jit(solution)/shard_map/ppermute | solution.py:186
  111.5 0.7 collective-permute-done.3.other_ref
  112.2 0.0 copy-done.2
  112.2 0.0 copy-start.6
  112.2 1.0 copy-done.6
  113.3 4.4 %finish.1 = (f32[512,128]{1,0:T(8,128)}, f32[1024,128]{1,0:T(8,128)}) custom-call(f32[512,512]{1,0:T(8,128)S(1)} %get-tuple-element.17.w_ref, f32[128,256]{1,0:T(8,128)S(1)} %reduce_sum.29.kept_ref, f32[128,256]{1,0:T(8,128)S(1)} %collective-permute-done.3.other_ref, f32[1024,512]{1,0:T(8,128)S(1)} %copy-done.2, f32[1024,128]{1,0:T(8,128)S(1)} %copy-done.6, ...), custom_call_target="tpu_custom_call" | custom-call | tf_op jit(solution)/shard_map/finish/pallas_call | solution.py:253
  (6 shorter events, 0.1 us)
Async XLA Ops:
  7.2 57.3 %all-gather.2.cloned.1.call-start = ((), (), s32[]{:S(2)}) async-start(), calls=%async_computation.5 | async-start | bytes 2359296 | tf_op jit(solution)/shard_map/all_gather | solution.py:272
  8.1 56.4 %copy-start.5 = (f32[1024,128]{1,0:T(8,128)S(1)}, f32[1024,128]{1,0:T(8,128)}, u32[]{:S(2)}) copy-start(f32[1024,128]{1,0:T(8,128)} %t_ref.3) | copy-start | bytes 1572868
  18.5 1.0 copy-start
  38.2 6.1 %collective-permute-start = (f32[40,128]{1,0:T(8,128)S(1)}, f32[40,128]{1,0:T(8,128)S(1)}, u32[]{:S(2)}, u32[]{:S(2)}) collective-permute-start(f32[40,128]{1,0:T(8,128)S(1)} %reduce_sum.27), channel_id=1, source_target_pairs={{0,256},{256,0},{1,257},{257,1},{2,258},{258,2},{3,259},{259,3},{4... | collective-permute-start | bytes 61448 | tf_op jit(solution)/shard_map/ppermute | solution.py:186
  60.6 21.7 %all-to-all-start.3 = ((f32[32,40,128]{2,1,0:T(8,128)}), f32[32,40,128]{2,1,0:T(8,128)S(1)}, u32[]{:S(2)}, u32[]{:S(2)}) async-start(f32[32,40,128]{2,1,0:T(8,128)} %broadcast_in_dim.10), calls=%async_computation.3 | async-start | bytes 1310720 | tf_op jit(solution)/shard_map/all_to_all | solution.py:182
  64.5 1.6 %copy-start.1 = (f32[1024,512]{1,0:T(8,128)S(1)}, f32[1024,512]{1,0:T(8,128)}, u32[]{:S(2)}) copy-start(f32[1024,512]{1,0:T(8,128)} %all-gather.2.cloned.1.call-done.p_ref) | copy-start | bytes 6291460
  67.2 6.6 %collective-permute-start.1 = (f32[128,256]{1,0:T(8,128)S(1)}, f32[128,256]{1,0:T(8,128)S(1)}, u32[]{:S(2)}, u32[]{:S(2)}) collective-permute-start(f32[128,256]{1,0:T(8,128)S(1)} %get-tuple-element.15), channel_id=1, source_target_pairs={{0,256},{256,0},{1,257},{257,1},{2,258},{258,2},{3,259},{259,3},{4... | collective-permute-start | bytes 393224 | tf_op jit(solution)/shard_map/ppermute | solution.py:186
  73.9 6.6 %collective-permute-start.2 = (f32[128,256]{1,0:T(8,128)S(1)}, f32[128,256]{1,0:T(8,128)S(1)}, u32[]{:S(2)}, u32[]{:S(2)}) collective-permute-start(f32[128,256]{1,0:T(8,128)S(1)} %add.10), channel_id=1, source_target_pairs={{0,32},{32,0},{64,96},{96,64},{128,160},{160,128},{192,224},{224,1... | collective-permute-start | bytes 393224 | tf_op jit(solution)/shard_map/ppermute | solution.py:283
  82.3 1.0 copy-start.3
  83.3 23.5 %all-to-all-start.4 = ((f32[4,128,256]{2,1,0:T(8,128)}), f32[4,128,256]{2,1,0:T(8,128)}, u32[]{:S(2)}, u32[]{:S(2)}) async-start(f32[4,128,256]{2,1,0:T(8,128)} %broadcast_in_dim.11), calls=%async_computation.4 | async-start | bytes 1048576 | tf_op jit(solution)/shard_map/all_to_all | solution.py:182
  91.6 1.1 copy-start.4
  92.7 19.6 %copy-start.2 = (f32[1024,512]{1,0:T(8,128)S(1)}, f32[1024,512]{1,0:T(8,128)}, u32[]{:S(2)}) copy-start(f32[1024,512]{1,0:T(8,128)} %all-gather.2.cloned.1.call-done.p_ref) | copy-start | bytes 6291460
  107.9 4.3 %collective-permute-start.3 = (f32[128,256]{1,0:T(8,128)S(1)}, f32[128,256]{1,0:T(8,128)S(1)}, u32[]{:S(2)}, u32[]{:S(2)}) collective-permute-start(f32[128,256]{1,0:T(8,128)S(1)} %reduce_sum.29.kept_ref), channel_id=1, source_target_pairs={{0,256},{256,0},{1,257},{257,1},{2,258},{258,2},{3,259},{259,3},{4... | collective-permute-start | bytes 393224 | tf_op jit(solution)/shard_map/ppermute | solution.py:186
  112.2 1.0 copy-start.6
Sparse Core Ops, SparseCore 0:
  18.6 44.8 all-gather.1

commit v5 on v4

--- a/solution.py
+++ b/solution.py
@@ -12,9 +12,9 @@
 NP = B // V
 X = 4
 Z = 8
-PARTS = 4
+ROWS = 32
 GROUP = 4
-SHARE_ROWS = B // X
+SHARE_ROWS = B // Z
 HI = lax.Precision.HIGHEST
 F32 = jnp.float32
 BF16 = jnp.bfloat16
@@ -124,11 +124,11 @@
 
 
 def tile(g_ref, block, t):
-    s = block * SHARE_ROWS + t % 4 * V
-    return g_ref[s // 40 * X + t // 4, s % 40 : s % 40 + V, :]
-
-
-def factor_kernel(g_ref, after_ref, r_ref, w_ref, end_ref, m_ref):
+    s = block * SHARE_ROWS + t % 2 * V
+    return g_ref[t // 2 * X + s // 40, s % 40 : s % 40 + V, :]
+
+
+def factor_kernel(g_ref, after_ref, r_ref, w_ref, m_ref):
     block = 0
     for i in range(NB):
         for j in range(i, NB):
@@ -159,17 +159,16 @@
             if k:
                 m_ref[e:, :o] = m_ref[e:, :o] - dot(p_left, right(wl, 0), ((0,), (0,)))
             m_ref[e:, o:e] = -dot(p_left, right(v, 0), ((0,), (0,)))
-    end_ref[...] = jnp.zeros_like(end_ref)
 
 
 def factor(shares, after):
     out = jax.ShapeDtypeStruct((N, N), F32)
     return pl.pallas_call(
         factor_kernel,
-        out_shape=(out, out, jax.ShapeDtypeStruct((V, B), F32)),
+        out_shape=(out, out),
         scratch_shapes=[pltpu.VMEM((N, N), F32)],
         in_specs=[VMEM, pl.BlockSpec(memory_space=pl.ANY)],
-        out_specs=(VMEM, VMEM, VMEM),
+        out_specs=(VMEM, VMEM),
         compiler_params=PARAMS,
         cost_estimate=pl.CostEstimate(flops=20_000_000_000, bytes_accessed=3 * 2**20, transcendentals=0),
         name="factor",
@@ -187,7 +186,7 @@
 
 
 def gram_kernel(p_ref, own_ref, t_ref):
-    first = lax.axis_index("dev") % X * SHARE_ROWS
+    first = lax.axis_index("dev") // X * SHARE_ROWS
     for i in range(NB):
         t_ref[i * B : (i + 1) * B, :] = p_ref[:, i * B : (i + 1) * B].T
     left = jnp.concatenate([t_ref[pl.ds(pl.multiple_of(i * B + first, SHARE_ROWS), SHARE_ROWS), :] for i in range(NB)], 0)
@@ -204,7 +203,7 @@
 def gram_shares(rows):
     return pl.pallas_call(
         gram_kernel,
-        out_shape=jax.ShapeDtypeStruct((Z, 40, B), F32),
+        out_shape=jax.ShapeDtypeStruct((X, 40, B), F32),
         scratch_shapes=[pltpu.VMEM((N, rows.shape[0]), F32)],
         in_specs=[VMEM],
         out_specs=VMEM,
@@ -213,12 +212,16 @@
     )(rows)
 
 
-def cross_kernel(p_ref, t_ref, kept_ref, given_ref):
-    rows = p_ref.shape[0] // PARTS
+def slab_rows(k, z):
+    x = (lax.axis_index("dev") + (X - k)) % X
+    return pl.ds(pl.multiple_of((z * X + x) * ROWS, ROWS), ROWS)
+
+
+def cross_kernel(p0, p1, p2, p3, t_ref, kept_ref, given_ref):
     product = None
-    for i in range(PARTS):
-        here = slice(i * rows, (i + 1) * rows)
-        part = mm(t_ref[here, :].T, p_ref[here, :])
+    for k, p_ref in enumerate((p0, p1, p2, p3)):
+        t = jnp.concatenate([t_ref[slab_rows(k, z), :] for z in range(Z)], 0)
+        part = mm(t.T, p_ref[...])
         product = part if product is None else product + part
     first = lax.axis_index("half") == 0
     low, high = product[:, : N // 2], product[:, N // 2 :]
@@ -226,67 +229,75 @@
     given_ref[...] = jnp.where(first, high, low)
 
 
-def cross_halves(panel_group, trailing):
+def cross_halves(blocks, trailing):
     out = jax.ShapeDtypeStruct((trailing.shape[1], N // 2), F32)
     return pl.pallas_call(
         cross_kernel,
         out_shape=(out, out),
-        in_specs=[VMEM] * 2,
-        out_specs=(VMEM,) * 2,
+        in_specs=[VMEM] * 5,
+        out_specs=(VMEM, VMEM),
         compiler_params=PARAMS,
         cost_estimate=pl.CostEstimate(flops=2_000_000_000, bytes_accessed=3 * 2**20, transcendentals=0),
         name="cross",
-    )(panel_group, trailing)
-
-
-def finish_kernel(w_ref, kept_ref, other_ref, p_ref, t_ref, end_ref, y_ref, r_ref):
+    )(*blocks, trailing)
+
+
+def finish_kernel(w_ref, kept_ref, other_ref, p0, p1, p2, p3, t_ref, y_ref, r_ref):
     first = lax.axis_index("half") == 0
     kept, other = kept_ref[...], other_ref[...]
     cross = jnp.concatenate([jnp.where(first, kept, other), jnp.where(first, other, kept)], 1)
     projected = mm(cross, w_ref[...], ((1,), (1,)))
     y_ref[...] = projected.T
     solved = mm(projected, w_ref[...])
-    r_ref[...] = t_ref[...] - mm(p_ref[...], solved, ((1,), (1,)))
-
-
-def finish(inverse, kept, other, panel_group, trailing, end):
+    for k, p_ref in enumerate((p0, p1, p2, p3)):
+        part = mm(p_ref[...], solved, ((1,), (1,)))
+        for z in range(Z):
+            here = slab_rows(k, z)
+            r_ref[here, :] = t_ref[here, :] - part[z * ROWS : (z + 1) * ROWS, :]
+
+
+def finish(inverse, kept, other, blocks, trailing):
     return pl.pallas_call(
         finish_kernel,
         out_shape=(
             jax.ShapeDtypeStruct((N, trailing.shape[1]), F32),
             jax.ShapeDtypeStruct(trailing.shape, F32),
         ),
-        in_specs=[VMEM] * 6,
+        in_specs=[VMEM] * 8,
         out_specs=(VMEM, VMEM),
         compiler_params=PARAMS,
         name="finish",
-    )(inverse, kept, other, panel_group, trailing, end)
+    )(inverse, kept, other, *blocks, trailing)
+
+
+def paired(x, k):
+    groups = lax.axis_size("grp")
+    return x + lax.ppermute(x, "grp", [(g, g ^ k) for g in range(groups)])
 
 
 def on_device(panel_block, trailing):
     along_x = [[z * X + x for x in range(X)] for z in range(Z)]
     along_z = [[z * X + x for z in range(Z)] for x in range(X)]
-    groups = lax.axis_size("grp")
-    alternate = [list(range(first, groups, 2)) for first in range(2)]
-    rows = sent_to_all(panel_block, "dev", along_x).reshape(-1, N)
-    panel_group = lax.all_gather(rows, "dev", axis=0, axis_index_groups=along_z, tiled=True)
+    rows = sent_to_all(panel_block, "dev", along_z).reshape(-1, N)
 
     own = gram_shares(rows)
-    share = lax.all_to_all(own, "dev", 0, 0, axis_index_groups=along_z, tiled=True).sum(0)
+    share = lax.all_to_all(own, "dev", 0, 0, axis_index_groups=along_x, tiled=True).sum(0)
+    rows, _ = lax.optimization_barrier((rows, own))
+    blocks = [rows]
+    for k in range(1, X):
+        moves = [(z * X + x, z * X + (x + k) % X) for z in range(Z) for x in range(X)]
+        blocks.append(lax.ppermute(rows, "dev", moves))
     share = share + swapped(share)
+    blocks[0], _ = lax.optimization_barrier((blocks[0], share))
     share = sent_to_all(share, "grp").sum(0)
+
+    kept, given = cross_halves(blocks, trailing)
+    kept = paired(kept + swapped(given), 1)
+    share, kept = lax.optimization_barrier((share, kept))
     shares = sent_to_all(share, "dev")
-
-    panel_group, _ = lax.optimization_barrier((panel_group, share))
-    kept, given = cross_halves(panel_group, trailing)
-    kept = kept + swapped(given)
-    kept = kept + lax.ppermute(kept, "grp", [(g, g ^ 1) for g in range(groups)])
-
-    triangle, inverse, end = factor(shares, kept)
-    kept = sent_to_all(kept, "grp", alternate).sum(0)
-    kept, end = lax.optimization_barrier((kept, end))
-    other = swapped(kept)
-    projected, remainder = finish(inverse, kept, other, panel_group, trailing, end)
+    kept = paired(paired(kept, 2), 4)
+    triangle, inverse = factor(shares, kept)
+    projected, remainder = finish(inverse, kept, swapped(kept), blocks, trailing)
     return (triangle, projected, remainder)
 
 

time: 125 us -> 136 us (1.088)
  starting transfers between devices: 29.9 us -> 51 us
  between operations: 14.2 us -> 0.8 us
  waiting for transfers between devices: 7.8 us -> 14.1 us
  local copies, waits for them, and re-layouts: 7.43 us -> 2.45 us
  blocking collectives: 43.9 us -> 46.4 us
    ppermute x1 -> x6, starting transfers between devices: 3.11 us -> 25.7 us  [the longest x3 15 us: paired(): return x + lax.ppermute(x, 'grp', [(g, g ^ k) for g in range(groups)])]
    ppermute x1 -> x6, waiting for transfers between devices: 3.49 us -> 12.1 us  [the longest x3 12 us: paired(): return x + lax.ppermute(x, 'grp', [(g, g ^ k) for g in range(groups)])]
    unnamed x14 -> x2, local copies, waits for them, and re-layouts: 4.78 us -> 0.01 us
    all_to_all x1, blocking collectives: 18.3 us -> 19.8 us  [on_device(): lax.all_to_all(own, 'dev', 0, 0, axis_index_groups=along_x, tiled=True)]
    ppermute x3, starting transfers between devices: 14.5 us -> 13.1 us  [swapped(): return lax.ppermute(x, 'half', [(0, 1), (1, 0)])]
    all_to_all x2, waiting for transfers between devices: 1.73 us -> 0.27 us  [sent_to_all(): lax.all_to_all(copies, axis, 0, 0, axis_index_groups=groups, tiled=True)]
    all_to_all x2 -> x1, blocking collectives: 25.7 us -> 26.7 us  [sent_to_all(): lax.all_to_all(copies, axis, 0, 0, axis_index_groups=groups, tiled=True)]
  transfers between devices with their start and end apart: 7 -> 11, of which waited for: 5 -> 6; matrix products, arithmetic and copies ran while one was open for 1% -> 1% of each run, Pallas kernels for 13% -> 11%
where the time goes in v5:
time: 136 us; the launch traced here: 135 us
  starting transfers between devices  51 us (38%)
  blocking collectives  46.4 us (34%)
  Pallas kernels  20.2 us (15%)
  waiting for transfers between devices  14.1 us (10%)
  local copies, waits for them, and re-layouts  2.45 us (2%)
    all_to_all x1, blocking collectives, sent_to_all(): lax.all_to_all(copies, axis, 0, 0, axis_index_groups=groups, tiled=True)  26.7 us
    all_to_all x1, blocking collectives, on_device(): lax.all_to_all(own, 'dev', 0, 0, axis_index_groups=along_x, tiled=True)  19.8 us
    ppermute x3, starting transfers between devices, paired(): return x + lax.ppermute(x, 'grp', [(g, g ^ k) for g in range(groups)])  15 us
    pallas_call x1, Pallas kernels, factor(): pl.pallas_call(factor_kernel, out_shape=(out, out), scratch_shapes=[pltpu...  14.1 us
    ppermute x3, starting transfers between devices, swapped(): return lax.ppermute(x, 'half', [(0, 1), (1, 0)])  13.1 us
    all_to_all x2, starting transfers between devices, sent_to_all(): lax.all_to_all(copies, axis, 0, 0, axis_index_groups=groups, tiled=True)  12.3 us
    ppermute x3, waiting for transfers between devices, paired(): return x + lax.ppermute(x, 'grp', [(g, g ^ k) for g in range(groups)])  12 us
    ppermute x3, starting transfers between devices, on_device(): blocks.append(lax.ppermute(rows, 'dev', moves))  10.7 us
  transfers between devices with their start and end apart: 11, of which 6 were waited for; matrix products, arithmetic and copies ran while one was open for 1% of the time, Pallas kernels for 11%

profile of v5, /device:TPU:1, one launch (start us, length us, event | category | flops | bytes accessed | tf_op | source)
XLA Modules:
  0.0 135.1 jit_solution(9602826162352833610)
XLA Ops:
  0.6 0.9 broadcast_in_dim.6
  1.5 26.7 %all_to_all.20 = f32[8,32,512]{2,1,0:T(8,128)S(1)} all-to-all(f32[8,32,512]{2,1,0:T(8,128)S(1)} %broadcast_in_dim.6), channel_id=1, replica_groups={{0,4,8,12,16,20,24,28},{1,5,9,13,17,21,25,29},{2,6,10,14,18,22,26,30},{..., dimensions={0} | all-to-all | bytes 1048576 | tf_op jit(solution)/shard_map/all_to_all | solution.py:181
  28.2 0.6 gram.1
  28.8 0.0 copy-start
  28.8 3.3 %collective-permute-start.1 = (f32[256,512]{1,0:T(8,128)S(1)}, f32[256,512]{1,0:T(8,128)S(1)}, u32[]{:S(2)}, u32[]{:S(2)}) collective-permute-start(f32[256,512]{1,0:T(8,128)S(1)} %bitcast.2), channel_id=1, source_target_pairs={{0,1},{1,2},{2,3},{3,0},{4,5},{5,6},{6,7},{7,4},{8,9},{9,10},{10,1... | collective-permute-start | bytes 1572872 | tf_op jit(solution)/shard_map/ppermute | solution.py:289
  32.0 4.4 %collective-permute-start.2 = (f32[256,512]{1,0:T(8,128)S(1)}, f32[256,512]{1,0:T(8,128)S(1)}, u32[]{:S(2)}, u32[]{:S(2)}) collective-permute-start(f32[256,512]{1,0:T(8,128)S(1)} %bitcast.3), channel_id=1, source_target_pairs={{0,2},{1,3},{2,0},{3,1},{4,6},{5,7},{6,4},{7,5},{8,10},{9,11},{10,... | collective-permute-start | bytes 1572872 | tf_op jit(solution)/shard_map/ppermute | solution.py:289
  36.4 3.1 %collective-permute-start.3 = (f32[256,512]{1,0:T(8,128)S(1)}, f32[256,512]{1,0:T(8,128)S(1)}, u32[]{:S(2)}, u32[]{:S(2)}) collective-permute-start(f32[256,512]{1,0:T(8,128)S(1)} %bitcast.4), channel_id=1, source_target_pairs={{0,3},{1,0},{2,1},{3,2},{4,7},{5,4},{6,5},{7,6},{8,11},{9,8},{10,9... | collective-permute-start | bytes 1572872 | tf_op jit(solution)/shard_map/ppermute | solution.py:289
  39.5 19.8 %all_to_all.21 = f32[4,40,128]{2,1,0:T(8,128)S(1)} all-to-all(f32[4,40,128]{2,1,0:T(8,128)S(1)} %gram.1), channel_id=1, replica_groups={{0,1,2,3},{4,5,6,7},{8,9,10,11},{12,13,14,15},{16,17,18,19},{20,21,22,2..., dimensions={0} | all-to-all | bytes 163840 | tf_op jit(solution)/shard_map/all_to_all | solution.py:284
  59.2 3.5 %collective-permute-start = (f32[40,128]{1,0:T(8,128)S(1)}, f32[40,128]{1,0:T(8,128)S(1)}, u32[]{:S(2)}, u32[]{:S(2)}) collective-permute-start(f32[40,128]{1,0:T(8,128)S(1)} %reduce_sum.18), channel_id=1, source_target_pairs={{0,256},{256,0},{1,257},{257,1},{2,258},{258,2},{3,259},{259,3},{4... | collective-permute-start | bytes 61448 | tf_op jit(solution)/shard_map/ppermute | solution.py:185
  62.7 0.8 collective-permute-done
  63.5 0.7 broadcast_in_dim.7
  64.2 6.8 %all-to-all-start.2 = ((f32[8,40,128]{2,1,0:T(8,128)}), f32[8,40,128]{2,1,0:T(8,128)S(1)}, u32[]{:S(2)}, u32[]{:S(2)}) async-start(f32[8,40,128]{2,1,0:T(8,128)} %broadcast_in_dim.7), calls=%async_computation.2 | async-start | bytes 327680 | tf_op jit(solution)/shard_map/all_to_all | solution.py:181
  71.0 0.0 collective-permute-done.1.p1
  71.0 0.0 collective-permute-done.2.p2
  71.1 0.0 collective-permute-done.3.p3
  71.1 0.0 copy-done
  71.1 1.2 cross.1
  72.2 2.5 %collective-permute-start.4 = (f32[128,256]{1,0:T(8,128)S(1)}, f32[128,256]{1,0:T(8,128)S(1)}, u32[]{:S(2)}, u32[]{:S(2)}) collective-permute-start(f32[128,256]{1,0:T(8,128)S(1)} %get-tuple-element.16), channel_id=1, source_target_pairs={{0,256},{256,0},{1,257},{257,1},{2,258},{258,2},{3,259},{259,3},{4... | collective-permute-start | bytes 393224 | tf_op jit(solution)/shard_map/ppermute | solution.py:185
  74.8 1.0 collective-permute-done.4
  75.8 3.6 %collective-permute-start.5 = (f32[128,256]{1,0:T(8,128)S(1)}, f32[128,256]{1,0:T(8,128)S(1)}, u32[]{:S(2)}, u32[]{:S(2)}) collective-permute-start(f32[128,256]{1,0:T(8,128)S(1)} %add.16), channel_id=1, source_target_pairs={{0,32},{32,0},{64,96},{96,64},{128,160},{160,128},{192,224},{224,1... | collective-permute-start | bytes 393224 | tf_op jit(solution)/shard_map/ppermute | solution.py:275
  79.4 0.3 all-to-all-done.2
  79.7 3.3 %collective-permute-done.5 = f32[128,256]{1,0:T(8,128)S(1)} collective-permute-done((f32[128,256]{1,0:T(8,128)S(1)}, f32[128,256]{1,0:T(8,128)S(1)}, u32[]{:S(2)}, u32[]{:S(2)}) %collective-permute-start.5) | collective-permute-done | bytes 131104 | tf_op jit(solution)/shard_map/ppermute | solution.py:275
  83.0 0.9 broadcast_in_dim.8
  83.9 5.5 %all-to-all-start.3 = ((f32[32,40,128]{2,1,0:T(8,128)}), f32[32,40,128]{2,1,0:T(8,128)S(1)}, u32[]{:S(2)}, u32[]{:S(2)}) async-start(f32[32,40,128]{2,1,0:T(8,128)} %broadcast_in_dim.8), calls=%async_computation.3 | async-start | bytes 1310720 | tf_op jit(solution)/shard_map/all_to_all | solution.py:181
  89.4 4.0 %collective-permute-start.6 = (f32[128,256]{1,0:T(8,128)S(1)}, f32[128,256]{1,0:T(8,128)S(1)}, u32[]{:S(2)}, u32[]{:S(2)}) collective-permute-start(f32[128,256]{1,0:T(8,128)S(1)} %add.17), channel_id=1, source_target_pairs={{0,64},{32,96},{64,0},{96,32},{128,192},{160,224},{192,128},{224,1... | collective-permute-start | bytes 393224 | tf_op jit(solution)/shard_map/ppermute | solution.py:275
  93.3 6.1 %collective-permute-done.6 = f32[128,256]{1,0:T(8,128)S(1)} collective-permute-done((f32[128,256]{1,0:T(8,128)S(1)}, f32[128,256]{1,0:T(8,128)S(1)}, u32[]{:S(2)}, u32[]{:S(2)}) %collective-permute-start.6) | collective-permute-done | bytes 131104 | tf_op jit(solution)/shard_map/ppermute | solution.py:275
  99.5 7.4 %collective-permute-start.7 = (f32[128,256]{1,0:T(8,128)S(1)}, f32[128,256]{1,0:T(8,128)S(1)}, u32[]{:S(2)}, u32[]{:S(2)}) collective-permute-start(f32[128,256]{1,0:T(8,128)S(1)} %add.18), channel_id=1, source_target_pairs={{0,128},{32,160},{64,192},{96,224},{128,0},{160,32},{192,64},{224,... | collective-permute-start | bytes 393224 | tf_op jit(solution)/shard_map/ppermute | solution.py:275
  106.9 2.6 %collective-permute-done.7 = f32[128,256]{1,0:T(8,128)S(1)} collective-permute-done((f32[128,256]{1,0:T(8,128)S(1)}, f32[128,256]{1,0:T(8,128)S(1)}, u32[]{:S(2)}, u32[]{:S(2)}) %collective-permute-start.7) | collective-permute-done | bytes 131104 | tf_op jit(solution)/shard_map/ppermute | solution.py:275
  109.6 7.1 %collective-permute-start.8 = (f32[128,256]{1,0:T(8,128)S(1)}, f32[128,256]{1,0:T(8,128)S(1)}, u32[]{:S(2)}, u32[]{:S(2)}) collective-permute-start(f32[128,256]{1,0:T(8,128)S(1)} %add.19.after_ref.kept_ref), channel_id=1, source_target_pairs={{0,256},{256,0},{1,257},{257,1},{2,258},{258,2},{3,259},{259,3},{4... | collective-permute-start | bytes 393224 | tf_op jit(solution)/shard_map/ppermute | solution.py:185
  116.6 0.0 all-to-all-done.3.g_ref
  116.6 14.1 %factor.1 = (f32[512,512]{1,0:T(8,128)}, f32[512,512]{1,0:T(8,128)S(1)}) custom-call(f32[32,40,128]{2,1,0:T(8,128)S(1)} %all-to-all-done.3.g_ref, f32[128,256]{1,0:T(8,128)S(1)} %add.19.after_ref.kept_ref), custom_call_target="tpu_custom_call" | custom-call | flops 20000000000 | bytes 3145728 | tf_op jit(solution)/shard_map/factor/pallas_call | solution.py:166
  130.8 0.0 collective-permute-done.8.other_ref
  130.8 4.3 %finish.1 = (f32[512,128]{1,0:T(8,128)}, f32[1024,128]{1,0:T(8,128)}) custom-call(f32[512,512]{1,0:T(8,128)S(1)} %get-tuple-element.20.w_ref, f32[128,256]{1,0:T(8,128)S(1)} %add.19.after_ref.kept_ref, f32[128,256]{1,0:T(8,128)S(1)} %collective-permute-done.8.other_ref, f32[256,512]{1,0:T(8,128)S(1)} %bitcast.6, f32[256,512]{1,0:T(8,128)S(1)} %collective-permute-done.1.p1, ...), custom_call_target="tpu_custom_call" | custom-call | tf_op jit(solution)/shard_map/finish/pallas_call | solution.py:260
  (7 shorter events, 0.1 us)
Async XLA Ops:
  28.8 42.3 %copy-start = (f32[1024,128]{1,0:T(8,128)S(1)}, f32[1024,128]{1,0:T(8,128)}, u32[]{:S(2)}) copy-start(f32[1024,128]{1,0:T(8,128)} %t_ref.3) | copy-start | bytes 1572868
  28.8 42.3 %collective-permute-start.1 = (f32[256,512]{1,0:T(8,128)S(1)}, f32[256,512]{1,0:T(8,128)S(1)}, u32[]{:S(2)}, u32[]{:S(2)}) collective-permute-start(f32[256,512]{1,0:T(8,128)S(1)} %bitcast.2), channel_id=1, source_target_pairs={{0,1},{1,2},{2,3},{3,0},{4,5},{5,6},{6,7},{7,4},{8,9},{9,10},{10,1... | collective-permute-start | bytes 1572872 | tf_op jit(solution)/shard_map/ppermute | solution.py:289
  32.0 39.0 %collective-permute-start.2 = (f32[256,512]{1,0:T(8,128)S(1)}, f32[256,512]{1,0:T(8,128)S(1)}, u32[]{:S(2)}, u32[]{:S(2)}) collective-permute-start(f32[256,512]{1,0:T(8,128)S(1)} %bitcast.3), channel_id=1, source_target_pairs={{0,2},{1,3},{2,0},{3,1},{4,6},{5,7},{6,4},{7,5},{8,10},{9,11},{10,... | collective-permute-start | bytes 1572872 | tf_op jit(solution)/shard_map/ppermute | solution.py:289
  36.4 34.7 %collective-permute-start.3 = (f32[256,512]{1,0:T(8,128)S(1)}, f32[256,512]{1,0:T(8,128)S(1)}, u32[]{:S(2)}, u32[]{:S(2)}) collective-permute-start(f32[256,512]{1,0:T(8,128)S(1)} %bitcast.4), channel_id=1, source_target_pairs={{0,3},{1,0},{2,1},{3,2},{4,7},{5,4},{6,5},{7,6},{8,11},{9,8},{10,9... | collective-permute-start | bytes 1572872 | tf_op jit(solution)/shard_map/ppermute | solution.py:289
  59.2 4.3 %collective-permute-start = (f32[40,128]{1,0:T(8,128)S(1)}, f32[40,128]{1,0:T(8,128)S(1)}, u32[]{:S(2)}, u32[]{:S(2)}) collective-permute-start(f32[40,128]{1,0:T(8,128)S(1)} %reduce_sum.18), channel_id=1, source_target_pairs={{0,256},{256,0},{1,257},{257,1},{2,258},{258,2},{3,259},{259,3},{4... | collective-permute-start | bytes 61448 | tf_op jit(solution)/shard_map/ppermute | solution.py:185
  64.2 15.5 %all-to-all-start.2 = ((f32[8,40,128]{2,1,0:T(8,128)}), f32[8,40,128]{2,1,0:T(8,128)S(1)}, u32[]{:S(2)}, u32[]{:S(2)}) async-start(f32[8,40,128]{2,1,0:T(8,128)} %broadcast_in_dim.7), calls=%async_computation.2 | async-start | bytes 327680 | tf_op jit(solution)/shard_map/all_to_all | solution.py:181
  72.2 3.5 %collective-permute-start.4 = (f32[128,256]{1,0:T(8,128)S(1)}, f32[128,256]{1,0:T(8,128)S(1)}, u32[]{:S(2)}, u32[]{:S(2)}) collective-permute-start(f32[128,256]{1,0:T(8,128)S(1)} %get-tuple-element.16), channel_id=1, source_target_pairs={{0,256},{256,0},{1,257},{257,1},{2,258},{258,2},{3,259},{259,3},{4... | collective-permute-start | bytes 393224 | tf_op jit(solution)/shard_map/ppermute | solution.py:185
  75.8 7.2 %collective-permute-start.5 = (f32[128,256]{1,0:T(8,128)S(1)}, f32[128,256]{1,0:T(8,128)S(1)}, u32[]{:S(2)}, u32[]{:S(2)}) collective-permute-start(f32[128,256]{1,0:T(8,128)S(1)} %add.16), channel_id=1, source_target_pairs={{0,32},{32,0},{64,96},{96,64},{128,160},{160,128},{192,224},{224,1... | collective-permute-start | bytes 393224 | tf_op jit(solution)/shard_map/ppermute | solution.py:275
  83.9 32.7 %all-to-all-start.3 = ((f32[32,40,128]{2,1,0:T(8,128)}), f32[32,40,128]{2,1,0:T(8,128)S(1)}, u32[]{:S(2)}, u32[]{:S(2)}) async-start(f32[32,40,128]{2,1,0:T(8,128)} %broadcast_in_dim.8), calls=%async_computation.3 | async-start | bytes 1310720 | tf_op jit(solution)/shard_map/all_to_all | solution.py:181
  89.4 10.1 %collective-permute-start.6 = (f32[128,256]{1,0:T(8,128)S(1)}, f32[128,256]{1,0:T(8,128)S(1)}, u32[]{:S(2)}, u32[]{:S(2)}) collective-permute-start(f32[128,256]{1,0:T(8,128)S(1)} %add.17), channel_id=1, source_target_pairs={{0,64},{32,96},{64,0},{96,32},{128,192},{160,224},{192,128},{224,1... | collective-permute-start | bytes 393224 | tf_op jit(solution)/shard_map/ppermute | solution.py:275
  99.5 10.0 %collective-permute-start.7 = (f32[128,256]{1,0:T(8,128)S(1)}, f32[128,256]{1,0:T(8,128)S(1)}, u32[]{:S(2)}, u32[]{:S(2)}) collective-permute-start(f32[128,256]{1,0:T(8,128)S(1)} %add.18), channel_id=1, source_target_pairs={{0,128},{32,160},{64,192},{96,224},{128,0},{160,32},{192,64},{224,... | collective-permute-start | bytes 393224 | tf_op jit(solution)/shard_map/ppermute | solution.py:275
  109.6 21.2 %collective-permute-start.8 = (f32[128,256]{1,0:T(8,128)S(1)}, f32[128,256]{1,0:T(8,128)S(1)}, u32[]{:S(2)}, u32[]{:S(2)}) collective-permute-start(f32[128,256]{1,0:T(8,128)S(1)} %add.19.after_ref.kept_ref), channel_id=1, source_target_pairs={{0,256},{256,0},{1,257},{257,1},{2,258},{258,2},{3,259},{259,3},{4... | collective-permute-start | bytes 393224 | tf_op jit(solution)/shard_map/ppermute | solution.py:185

commit v6 on v4

--- a/solution.py
+++ b/solution.py
@@ -13,7 +13,7 @@
 X = 4
 Z = 8
 PARTS = 4
-GROUP = 4
+GROUP = 8
 SHARE_ROWS = B // X
 HI = lax.Precision.HIGHEST
 F32 = jnp.float32
@@ -41,6 +41,21 @@
 def right(x, axis):
     h, m, l = three(x)
     return jnp.concatenate([h, m, h, m, l, h], axis)
+
+
+def two(x):
+    high = x.astype(BF16)
+    return high, (x - high.astype(F32)).astype(BF16)
+
+
+def left2(x, axis):
+    h, l = two(x)
+    return jnp.concatenate([h, h, l], axis)
+
+
+def right2(x, axis):
+    h, l = two(x)
+    return jnp.concatenate([h, l, h], axis)
 
 
 def dot(a, b, dims):
@@ -218,7 +233,7 @@
     product = None
     for i in range(PARTS):
         here = slice(i * rows, (i + 1) * rows)
-        part = mm(t_ref[here, :].T, p_ref[here, :])
+        part = dot(left2(t_ref[here, :].T, 1), right2(p_ref[here, :], 0), ((1,), (0,)))
         product = part if product is None else product + part
     first = lax.axis_index("half") == 0
     low, high = product[:, : N // 2], product[:, N // 2 :]
@@ -243,10 +258,11 @@
     first = lax.axis_index("half") == 0
     kept, other = kept_ref[...], other_ref[...]
     cross = jnp.concatenate([jnp.where(first, kept, other), jnp.where(first, other, kept)], 1)
-    projected = mm(cross, w_ref[...], ((1,), (1,)))
+    w = w_ref[...]
+    projected = dot(left2(cross, 1), right2(w, 1), ((1,), (1,)))
     y_ref[...] = projected.T
-    solved = mm(projected, w_ref[...])
-    r_ref[...] = t_ref[...] - mm(p_ref[...], solved, ((1,), (1,)))
+    solved = right2(dot(left2(projected, 1), right2(w, 0), ((1,), (0,))), 1)
+    r_ref[...] = t_ref[...] - dot(left2(p_ref[...], 1), solved, ((1,), (1,)))
 
 
 def finish(inverse, kept, other, panel_group, trailing, end):

time: 125 us -> 123 us (0.984)
  Pallas kernels: 20.1 us -> 17.5 us
    pallas_call x1, Pallas kernels: 4.37 us -> 2.76 us  [finish(): pl.pallas_call(finish_kernel, out_shape=(jax.ShapeDtypeStruct((N, trailin...]
  transfers between devices with their start and end apart: 7 -> 7, of which waited for: 5 -> 6; matrix products, arithmetic and copies ran while one was open for 1% -> 1% of each run, Pallas kernels for 13% -> 12%
where the time goes in v6:
time: 123 us; the launch traced here: 122 us
  blocking collectives  43.9 us (36%)
  starting transfers between devices  29 us (24%)
  Pallas kernels  17.5 us (14%)
  between operations  14.2 us (12%)
  waiting for transfers between devices  8.86 us (7%)
  local copies, waits for them, and re-layouts  7.43 us (6%)
    all_to_all x2, blocking collectives, sent_to_all(): lax.all_to_all(copies, axis, 0, 0, axis_index_groups=groups, tiled=True)  25.7 us
    all_to_all x1, blocking collectives, on_device(): lax.all_to_all(own, 'dev', 0, 0, axis_index_groups=along_z, tiled=True)  18.3 us
    ppermute x3, starting transfers between devices, swapped(): return lax.ppermute(x, 'half', [(0, 1), (1, 0)])  14.1 us
    pallas_call x1, Pallas kernels, factor(): pl.pallas_call(factor_kernel, out_shape=(out, out, jax.ShapeDtypeStruct((...  13.5 us
    all_to_all x2, starting transfers between devices, sent_to_all(): lax.all_to_all(copies, axis, 0, 0, axis_index_groups=groups, tiled=True)  11.8 us
    unnamed x14, local copies, waits for them, and re-layouts  4.78 us
    ppermute x1, waiting for transfers between devices, on_device(): kept = kept + lax.ppermute(kept, 'grp', [(g, g ^ 1) for g in range(groups)])  3.49 us
    ppermute x1, starting transfers between devices, on_device(): kept = kept + lax.ppermute(kept, 'grp', [(g, g ^ 1) for g in range(groups)])  3.12 us
  transfers between devices with their start and end apart: 7, of which 6 were waited for; matrix products, arithmetic and copies ran while one was open for 1% of the time, Pallas kernels for 12%

profile of v6, /device:TPU:1, one launch (start us, length us, event | category | flops | bytes accessed | tf_op | source)
XLA Modules:
  0.0 122.0 jit_solution(6424681844450666176)
XLA Ops:
  7.2 0.0 all-gather.2.cloned.1.call-start
  7.2 0.9 broadcast_in_dim.8
  8.1 0.0 copy-start.5
  8.1 10.4 %all_to_all.25 = f32[4,32,512]{2,1,0:T(8,128)} all-to-all(f32[4,32,512]{2,1,0:T(8,128)S(1)} %broadcast_in_dim.8), channel_id=1, replica_groups={{0,1,2,3},{4,5,6,7},{8,9,10,11},{12,13,14,15},{16,17,18,19},{20,21,22,2..., dimensions={0} | all-to-all | bytes 524288 | tf_op jit(solution)/shard_map/all_to_all | solution.py:197
  18.5 0.0 all-gather.2.cloned.1.call-update
  18.5 0.0 copy-start
  18.5 0.9 copy-done
  19.5 0.5 gram.1
  20.0 18.3 %all_to_all.26 = f32[8,40,128]{2,1,0:T(8,128)S(1)} all-to-all(f32[8,40,128]{2,1,0:T(8,128)S(1)} %gram.1), channel_id=1, replica_groups={{0,4,8,12,16,20,24,28},{1,5,9,13,17,21,25,29},{2,6,10,14,18,22,26,30},{..., dimensions={0} | all-to-all | bytes 327680 | tf_op jit(solution)/shard_map/all_to_all | solution.py:291
  38.2 5.3 %collective-permute-start = (f32[40,128]{1,0:T(8,128)S(1)}, f32[40,128]{1,0:T(8,128)S(1)}, u32[]{:S(2)}, u32[]{:S(2)}) collective-permute-start(f32[40,128]{1,0:T(8,128)S(1)} %reduce_sum.27), channel_id=1, source_target_pairs={{0,256},{256,0},{1,257},{257,1},{2,258},{258,2},{3,259},{259,3},{4... | collective-permute-start | bytes 61448 | tf_op jit(solution)/shard_map/ppermute | solution.py:201
  43.5 0.8 collective-permute-done
  44.4 15.3 %all_to_all.27 = f32[8,40,128]{2,1,0:T(8,128)S(1)} all-to-all(f32[8,40,128]{2,1,0:T(8,128)S(1)} %broadcast_in_dim.9), channel_id=1, replica_groups=mesh['half'=2,'grp'=8,'dev'=32] {'grp'}, dimensions={0} | all-to-all | bytes 327680 | tf_op jit(solution)/shard_map/all_to_all | solution.py:197
  59.7 0.9 broadcast_in_dim.10
  60.6 3.9 %all-to-all-start.3 = ((f32[32,40,128]{2,1,0:T(8,128)}), f32[32,40,128]{2,1,0:T(8,128)S(1)}, u32[]{:S(2)}, u32[]{:S(2)}) async-start(f32[32,40,128]{2,1,0:T(8,128)} %broadcast_in_dim.10), calls=%async_computation.3 | async-start | bytes 1310720 | tf_op jit(solution)/shard_map/all_to_all | solution.py:197
  64.5 0.0 all-gather.2.cloned.1.call-done.p_ref
  64.5 0.0 copy-done.5
  64.5 0.0 copy-start.1
  64.5 1.6 %copy-done.1 = f32[1024,512]{1,0:T(8,128)S(1)} copy-done((f32[1024,512]{1,0:T(8,128)S(1)}, f32[1024,512]{1,0:T(8,128)}, u32[]{:S(2)}) %copy-start.1) | copy-done | bytes 2097176
  66.1 0.7 cross.1
  66.8 5.6 %collective-permute-start.1 = (f32[128,256]{1,0:T(8,128)S(1)}, f32[128,256]{1,0:T(8,128)S(1)}, u32[]{:S(2)}, u32[]{:S(2)}) collective-permute-start(f32[128,256]{1,0:T(8,128)S(1)} %get-tuple-element.15), channel_id=1, source_target_pairs={{0,256},{256,0},{1,257},{257,1},{2,258},{258,2},{3,259},{259,3},{4... | collective-permute-start | bytes 393224 | tf_op jit(solution)/shard_map/ppermute | solution.py:201
  72.5 1.0 collective-permute-done.1
  73.5 3.1 %collective-permute-start.2 = (f32[128,256]{1,0:T(8,128)S(1)}, f32[128,256]{1,0:T(8,128)S(1)}, u32[]{:S(2)}, u32[]{:S(2)}) collective-permute-start(f32[128,256]{1,0:T(8,128)S(1)} %add.10), channel_id=1, source_target_pairs={{0,32},{32,0},{64,96},{96,64},{128,160},{160,128},{192,224},{224,1... | collective-permute-start | bytes 393224 | tf_op jit(solution)/shard_map/ppermute | solution.py:299
  76.6 3.5 %collective-permute-done.2 = f32[128,256]{1,0:T(8,128)S(1)} collective-permute-done((f32[128,256]{1,0:T(8,128)S(1)}, f32[128,256]{1,0:T(8,128)S(1)}, u32[]{:S(2)}, u32[]{:S(2)}) %collective-permute-start.2) | collective-permute-done | bytes 131104 | tf_op jit(solution)/shard_map/ppermute | solution.py:299
  80.1 2.1 %all-to-all-done.3.g_ref = f32[32,40,128]{2,1,0:T(8,128)S(1)} async-done(((f32[32,40,128]{2,1,0:T(8,128)}), f32[32,40,128]{2,1,0:T(8,128)S(1)}, u32[]{:S(2)}, u32[]{:S(2)}) %all-to-all-start.3) | async-done | bytes 655392 | tf_op jit(solution)/shard_map/all_to_all | solution.py:197
  82.3 0.0 copy-start.3
  82.3 0.9 broadcast_in_dim.11
  83.1 0.1 copy-done.3
  83.3 7.9 %all-to-all-start.4 = ((f32[4,128,256]{2,1,0:T(8,128)}), f32[4,128,256]{2,1,0:T(8,128)}, u32[]{:S(2)}, u32[]{:S(2)}) async-start(f32[4,128,256]{2,1,0:T(8,128)} %broadcast_in_dim.11), calls=%async_computation.4 | async-start | bytes 1048576 | tf_op jit(solution)/shard_map/all_to_all | solution.py:197
  91.2 0.0 copy-start.4
  91.2 1.1 copy-done.4
  92.3 0.0 copy-start.2
  92.3 13.5 %factor.1 = (f32[512,512]{1,0:T(8,128)}, f32[512,512]{1,0:T(8,128)S(1)}, f32[8,128]{1,0:T(8,128)S(1)}) custom-call(f32[32,40,128]{2,1,0:T(8,128)S(1)} %copy-done.4, f32[128,256]{1,0:T(8,128)S(1)} %add.11.after_ref), custom_call_target="tpu_custom_call" | custom-call | flops 20000000000 | bytes 3145728 | tf_op jit(solution)/shard_map/factor/pallas_call | solution.py:182
  105.7 0.4 all-to-all-done.4
  106.2 1.1 reduce_sum.29.kept_ref
  107.3 3.1 %collective-permute-start.3 = (f32[128,256]{1,0:T(8,128)S(1)}, f32[128,256]{1,0:T(8,128)S(1)}, u32[]{:S(2)}, u32[]{:S(2)}) collective-permute-start(f32[128,256]{1,0:T(8,128)S(1)} %reduce_sum.29.kept_ref), channel_id=1, source_target_pairs={{0,256},{256,0},{1,257},{257,1},{2,258},{258,2},{3,259},{259,3},{4... | collective-permute-start | bytes 393224 | tf_op jit(solution)/shard_map/ppermute | solution.py:201
  110.4 1.0 collective-permute-done.3.other_ref
  111.4 0.0 copy-done.2
  111.4 0.0 copy-start.6
  111.4 1.0 copy-done.6
  112.4 2.8 %finish.1 = (f32[512,128]{1,0:T(8,128)}, f32[1024,128]{1,0:T(8,128)}) custom-call(f32[512,512]{1,0:T(8,128)S(1)} %get-tuple-element.17.w_ref, f32[128,256]{1,0:T(8,128)S(1)} %reduce_sum.29.kept_ref, f32[128,256]{1,0:T(8,128)S(1)} %collective-permute-done.3.other_ref, f32[1024,512]{1,0:T(8,128)S(1)} %copy-done.2, f32[1024,128]{1,0:T(8,128)S(1)} %copy-done.6, ...), custom_call_target="tpu_custom_call" | custom-call | tf_op jit(solution)/shard_map/finish/pallas_call | solution.py:269
  (6 shorter events, 0.1 us)
Async XLA Ops:
  7.2 57.3 %all-gather.2.cloned.1.call-start = ((), (), s32[]{:S(2)}) async-start(), calls=%async_computation.5 | async-start | bytes 2359296 | tf_op jit(solution)/shard_map/all_gather | solution.py:288
  8.1 56.4 %copy-start.5 = (f32[1024,128]{1,0:T(8,128)S(1)}, f32[1024,128]{1,0:T(8,128)}, u32[]{:S(2)}) copy-start(f32[1024,128]{1,0:T(8,128)} %t_ref.3) | copy-start | bytes 1572868
  18.5 1.0 copy-start
  38.2 6.1 %collective-permute-start = (f32[40,128]{1,0:T(8,128)S(1)}, f32[40,128]{1,0:T(8,128)S(1)}, u32[]{:S(2)}, u32[]{:S(2)}) collective-permute-start(f32[40,128]{1,0:T(8,128)S(1)} %reduce_sum.27), channel_id=1, source_target_pairs={{0,256},{256,0},{1,257},{257,1},{2,258},{258,2},{3,259},{259,3},{4... | collective-permute-start | bytes 61448 | tf_op jit(solution)/shard_map/ppermute | solution.py:201
  60.6 21.7 %all-to-all-start.3 = ((f32[32,40,128]{2,1,0:T(8,128)}), f32[32,40,128]{2,1,0:T(8,128)S(1)}, u32[]{:S(2)}, u32[]{:S(2)}) async-start(f32[32,40,128]{2,1,0:T(8,128)} %broadcast_in_dim.10), calls=%async_computation.3 | async-start | bytes 1310720 | tf_op jit(solution)/shard_map/all_to_all | solution.py:197
  64.5 1.6 %copy-start.1 = (f32[1024,512]{1,0:T(8,128)S(1)}, f32[1024,512]{1,0:T(8,128)}, u32[]{:S(2)}) copy-start(f32[1024,512]{1,0:T(8,128)} %all-gather.2.cloned.1.call-done.p_ref) | copy-start | bytes 6291460
  66.8 6.6 %collective-permute-start.1 = (f32[128,256]{1,0:T(8,128)S(1)}, f32[128,256]{1,0:T(8,128)S(1)}, u32[]{:S(2)}, u32[]{:S(2)}) collective-permute-start(f32[128,256]{1,0:T(8,128)S(1)} %get-tuple-element.15), channel_id=1, source_target_pairs={{0,256},{256,0},{1,257},{257,1},{2,258},{258,2},{3,259},{259,3},{4... | collective-permute-start | bytes 393224 | tf_op jit(solution)/shard_map/ppermute | solution.py:201
  73.5 6.6 %collective-permute-start.2 = (f32[128,256]{1,0:T(8,128)S(1)}, f32[128,256]{1,0:T(8,128)S(1)}, u32[]{:S(2)}, u32[]{:S(2)}) collective-permute-start(f32[128,256]{1,0:T(8,128)S(1)} %add.10), channel_id=1, source_target_pairs={{0,32},{32,0},{64,96},{96,64},{128,160},{160,128},{192,224},{224,1... | collective-permute-start | bytes 393224 | tf_op jit(solution)/shard_map/ppermute | solution.py:299
  82.3 1.0 copy-start.3
  83.3 22.9 %all-to-all-start.4 = ((f32[4,128,256]{2,1,0:T(8,128)}), f32[4,128,256]{2,1,0:T(8,128)}, u32[]{:S(2)}, u32[]{:S(2)}) async-start(f32[4,128,256]{2,1,0:T(8,128)} %broadcast_in_dim.11), calls=%async_computation.4 | async-start | bytes 1048576 | tf_op jit(solution)/shard_map/all_to_all | solution.py:197
  91.2 1.1 copy-start.4
  92.3 19.1 %copy-start.2 = (f32[1024,512]{1,0:T(8,128)S(1)}, f32[1024,512]{1,0:T(8,128)}, u32[]{:S(2)}) copy-start(f32[1024,512]{1,0:T(8,128)} %all-gather.2.cloned.1.call-done.p_ref) | copy-start | bytes 6291460
  107.3 4.1 %collective-permute-start.3 = (f32[128,256]{1,0:T(8,128)S(1)}, f32[128,256]{1,0:T(8,128)S(1)}, u32[]{:S(2)}, u32[]{:S(2)}) collective-permute-start(f32[128,256]{1,0:T(8,128)S(1)} %reduce_sum.29.kept_ref), channel_id=1, source_target_pairs={{0,256},{256,0},{1,257},{257,1},{2,258},{258,2},{3,259},{259,3},{4... | collective-permute-start | bytes 393224 | tf_op jit(solution)/shard_map/ppermute | solution.py:201
  111.4 1.0 copy-start.6
Sparse Core Ops, SparseCore 0:
  18.6 44.8 all-gather.1

commit v7 on v6

--- a/solution.py
+++ b/solution.py
@@ -150,6 +150,12 @@
             for t in range(NP):
                 m_ref[i * B + V * t : i * B + V * (t + 1), j * B : (j + 1) * B] = tile(g_ref, block, t)
             block += 1
+    on_diagonal = lax.broadcasted_iota(jnp.int32, (B, B), 0) == lax.broadcasted_iota(jnp.int32, (B, B), 1)
+    diagonals = [jnp.where(on_diagonal, m_ref[i * B : (i + 1) * B, i * B : (i + 1) * B], 0.0) for i in range(NB)]
+    scale = lax.rsqrt(jnp.concatenate([jnp.sum(d, 0, keepdims=True) for d in diagonals], 1))
+    for i in range(NB):
+        here = slice(i * B, (i + 1) * B)
+        m_ref[here, i * B :] = m_ref[here, i * B :] * lax.rsqrt(jnp.sum(diagonals[i], 1, keepdims=True)) * scale[:, i * B :]
     for k in range(NB):
         o = k * B
         e = o + B
@@ -174,6 +180,8 @@
             if k:
                 m_ref[e:, :o] = m_ref[e:, :o] - dot(p_left, right(wl, 0), ((0,), (0,)))
             m_ref[e:, o:e] = -dot(p_left, right(v, 0), ((0,), (0,)))
+    r_ref[...] = r_ref[...] * (1.0 / scale)
+    w_ref[...] = w_ref[...] * scale
     end_ref[...] = jnp.zeros_like(end_ref)
 
 

time: 123 us -> 123 us (level)
  no operation moved by 1% of the time
where the time goes in v7:
time: 123 us; the launch traced here: 122 us
  blocking collectives  43.9 us (36%)
  starting transfers between devices  29.1 us (24%)
  Pallas kernels  17.7 us (14%)
  between operations  14.2 us (12%)
  waiting for transfers between devices  8.58 us (7%)
  local copies, waits for them, and re-layouts  7.43 us (6%)
    all_to_all x2, blocking collectives, sent_to_all(): lax.all_to_all(copies, axis, 0, 0, axis_index_groups=groups, tiled=True)  25.7 us
    all_to_all x1, blocking collectives, on_device(): lax.all_to_all(own, 'dev', 0, 0, axis_index_groups=along_z, tiled=True)  18.3 us
    ppermute x3, starting transfers between devices, swapped(): return lax.ppermute(x, 'half', [(0, 1), (1, 0)])  14.2 us
    pallas_call x1, Pallas kernels, factor(): pl.pallas_call(factor_kernel, out_shape=(out, out, jax.ShapeDtypeStruct((...  13.8 us
    all_to_all x2, starting transfers between devices, sent_to_all(): lax.all_to_all(copies, axis, 0, 0, axis_index_groups=groups, tiled=True)  11.8 us
    unnamed x14, local copies, waits for them, and re-layouts  4.78 us
    ppermute x1, waiting for transfers between devices, on_device(): kept = kept + lax.ppermute(kept, 'grp', [(g, g ^ 1) for g in range(groups)])  3.49 us
    ppermute x1, starting transfers between devices, on_device(): kept = kept + lax.ppermute(kept, 'grp', [(g, g ^ 1) for g in range(groups)])  3.12 us
  transfers between devices with their start and end apart: 7, of which 6 were waited for; matrix products, arithmetic and copies ran while one was open for 1% of the time, Pallas kernels for 12%

profile of v7, /device:TPU:1, one launch (start us, length us, event | category | flops | bytes accessed | tf_op | source)
XLA Modules:
  0.0 122.1 jit_solution(16104755696910291200)
XLA Ops:
  7.2 0.0 all-gather.2.cloned.1.call-start
  7.2 0.9 broadcast_in_dim.8
  8.1 0.0 copy-start.5
  8.1 10.4 %all_to_all.25 = f32[4,32,512]{2,1,0:T(8,128)} all-to-all(f32[4,32,512]{2,1,0:T(8,128)S(1)} %broadcast_in_dim.8), channel_id=1, replica_groups={{0,1,2,3},{4,5,6,7},{8,9,10,11},{12,13,14,15},{16,17,18,19},{20,21,22,2..., dimensions={0} | all-to-all | bytes 524288 | tf_op jit(solution)/shard_map/all_to_all | solution.py:205
  18.5 0.0 all-gather.2.cloned.1.call-update
  18.5 0.0 copy-start
  18.5 0.9 copy-done
  19.5 0.5 gram.1
  20.0 18.3 %all_to_all.26 = f32[8,40,128]{2,1,0:T(8,128)S(1)} all-to-all(f32[8,40,128]{2,1,0:T(8,128)S(1)} %gram.1), channel_id=1, replica_groups={{0,4,8,12,16,20,24,28},{1,5,9,13,17,21,25,29},{2,6,10,14,18,22,26,30},{..., dimensions={0} | all-to-all | bytes 327680 | tf_op jit(solution)/shard_map/all_to_all | solution.py:299
  38.2 5.3 %collective-permute-start = (f32[40,128]{1,0:T(8,128)S(1)}, f32[40,128]{1,0:T(8,128)S(1)}, u32[]{:S(2)}, u32[]{:S(2)}) collective-permute-start(f32[40,128]{1,0:T(8,128)S(1)} %reduce_sum.27), channel_id=1, source_target_pairs={{0,256},{256,0},{1,257},{257,1},{2,258},{258,2},{3,259},{259,3},{4... | collective-permute-start | bytes 61448 | tf_op jit(solution)/shard_map/ppermute | solution.py:209
  43.5 0.8 collective-permute-done
  44.4 15.3 %all_to_all.27 = f32[8,40,128]{2,1,0:T(8,128)S(1)} all-to-all(f32[8,40,128]{2,1,0:T(8,128)S(1)} %broadcast_in_dim.9), channel_id=1, replica_groups=mesh['half'=2,'grp'=8,'dev'=32] {'grp'}, dimensions={0} | all-to-all | bytes 327680 | tf_op jit(solution)/shard_map/all_to_all | solution.py:205
  59.7 0.9 broadcast_in_dim.10
  60.6 3.9 %all-to-all-start.3 = ((f32[32,40,128]{2,1,0:T(8,128)}), f32[32,40,128]{2,1,0:T(8,128)S(1)}, u32[]{:S(2)}, u32[]{:S(2)}) async-start(f32[32,40,128]{2,1,0:T(8,128)} %broadcast_in_dim.10), calls=%async_computation.3 | async-start | bytes 1310720 | tf_op jit(solution)/shard_map/all_to_all | solution.py:205
  64.5 0.0 all-gather.2.cloned.1.call-done.p_ref
  64.5 0.0 copy-done.5
  64.5 0.0 copy-start.1
  64.5 1.6 %copy-done.1 = f32[1024,512]{1,0:T(8,128)S(1)} copy-done((f32[1024,512]{1,0:T(8,128)S(1)}, f32[1024,512]{1,0:T(8,128)}, u32[]{:S(2)}) %copy-start.1) | copy-done | bytes 2097176
  66.1 0.7 cross.1
  66.8 5.6 %collective-permute-start.1 = (f32[128,256]{1,0:T(8,128)S(1)}, f32[128,256]{1,0:T(8,128)S(1)}, u32[]{:S(2)}, u32[]{:S(2)}) collective-permute-start(f32[128,256]{1,0:T(8,128)S(1)} %get-tuple-element.15), channel_id=1, source_target_pairs={{0,256},{256,0},{1,257},{257,1},{2,258},{258,2},{3,259},{259,3},{4... | collective-permute-start | bytes 393224 | tf_op jit(solution)/shard_map/ppermute | solution.py:209
  72.5 1.0 collective-permute-done.1
  73.5 3.1 %collective-permute-start.2 = (f32[128,256]{1,0:T(8,128)S(1)}, f32[128,256]{1,0:T(8,128)S(1)}, u32[]{:S(2)}, u32[]{:S(2)}) collective-permute-start(f32[128,256]{1,0:T(8,128)S(1)} %add.10), channel_id=1, source_target_pairs={{0,32},{32,0},{64,96},{96,64},{128,160},{160,128},{192,224},{224,1... | collective-permute-start | bytes 393224 | tf_op jit(solution)/shard_map/ppermute | solution.py:307
  76.6 3.5 %collective-permute-done.2 = f32[128,256]{1,0:T(8,128)S(1)} collective-permute-done((f32[128,256]{1,0:T(8,128)S(1)}, f32[128,256]{1,0:T(8,128)S(1)}, u32[]{:S(2)}, u32[]{:S(2)}) %collective-permute-start.2) | collective-permute-done | bytes 131104 | tf_op jit(solution)/shard_map/ppermute | solution.py:307
  80.1 2.1 %all-to-all-done.3.g_ref = f32[32,40,128]{2,1,0:T(8,128)S(1)} async-done(((f32[32,40,128]{2,1,0:T(8,128)}), f32[32,40,128]{2,1,0:T(8,128)S(1)}, u32[]{:S(2)}, u32[]{:S(2)}) %all-to-all-start.3) | async-done | bytes 655392 | tf_op jit(solution)/shard_map/all_to_all | solution.py:205
  82.3 0.0 copy-start.3
  82.3 0.9 broadcast_in_dim.11
  83.1 0.1 copy-done.3
  83.3 7.9 %all-to-all-start.4 = ((f32[4,128,256]{2,1,0:T(8,128)}), f32[4,128,256]{2,1,0:T(8,128)}, u32[]{:S(2)}, u32[]{:S(2)}) async-start(f32[4,128,256]{2,1,0:T(8,128)} %broadcast_in_dim.11), calls=%async_computation.4 | async-start | bytes 1048576 | tf_op jit(solution)/shard_map/all_to_all | solution.py:205
  91.2 0.0 copy-start.4
  91.2 1.1 copy-done.4
  92.3 0.0 copy-start.2
  92.3 13.8 %factor.1 = (f32[512,512]{1,0:T(8,128)}, f32[512,512]{1,0:T(8,128)S(1)}, f32[8,128]{1,0:T(8,128)S(1)}) custom-call(f32[32,40,128]{2,1,0:T(8,128)S(1)} %copy-done.4, f32[128,256]{1,0:T(8,128)S(1)} %add.11.after_ref), custom_call_target="tpu_custom_call" | custom-call | flops 20000000000 | bytes 3145728 | tf_op jit(solution)/shard_map/factor/pallas_call | solution.py:190
  106.0 0.2 all-to-all-done.4
  106.2 1.1 reduce_sum.29.kept_ref
  107.3 3.2 %collective-permute-start.3 = (f32[128,256]{1,0:T(8,128)S(1)}, f32[128,256]{1,0:T(8,128)S(1)}, u32[]{:S(2)}, u32[]{:S(2)}) collective-permute-start(f32[128,256]{1,0:T(8,128)S(1)} %reduce_sum.29.kept_ref), channel_id=1, source_target_pairs={{0,256},{256,0},{1,257},{257,1},{2,258},{258,2},{3,259},{259,3},{4... | collective-permute-start | bytes 393224 | tf_op jit(solution)/shard_map/ppermute | solution.py:209
  110.5 1.0 collective-permute-done.3.other_ref
  111.5 0.0 copy-done.2
  111.5 0.0 copy-start.6
  111.5 1.0 copy-done.6
  112.5 2.8 %finish.1 = (f32[512,128]{1,0:T(8,128)}, f32[1024,128]{1,0:T(8,128)}) custom-call(f32[512,512]{1,0:T(8,128)S(1)} %get-tuple-element.17.w_ref, f32[128,256]{1,0:T(8,128)S(1)} %reduce_sum.29.kept_ref, f32[128,256]{1,0:T(8,128)S(1)} %collective-permute-done.3.other_ref, f32[1024,512]{1,0:T(8,128)S(1)} %copy-done.2, f32[1024,128]{1,0:T(8,128)S(1)} %copy-done.6, ...), custom_call_target="tpu_custom_call" | custom-call | tf_op jit(solution)/shard_map/finish/pallas_call | solution.py:277
  (6 shorter events, 0.1 us)
Async XLA Ops:
  7.2 57.3 %all-gather.2.cloned.1.call-start = ((), (), s32[]{:S(2)}) async-start(), calls=%async_computation.5 | async-start | bytes 2359296 | tf_op jit(solution)/shard_map/all_gather | solution.py:296
  8.1 56.4 %copy-start.5 = (f32[1024,128]{1,0:T(8,128)S(1)}, f32[1024,128]{1,0:T(8,128)}, u32[]{:S(2)}) copy-start(f32[1024,128]{1,0:T(8,128)} %t_ref.3) | copy-start | bytes 1572868
  18.5 1.0 copy-start
  38.2 6.1 %collective-permute-start = (f32[40,128]{1,0:T(8,128)S(1)}, f32[40,128]{1,0:T(8,128)S(1)}, u32[]{:S(2)}, u32[]{:S(2)}) collective-permute-start(f32[40,128]{1,0:T(8,128)S(1)} %reduce_sum.27), channel_id=1, source_target_pairs={{0,256},{256,0},{1,257},{257,1},{2,258},{258,2},{3,259},{259,3},{4... | collective-permute-start | bytes 61448 | tf_op jit(solution)/shard_map/ppermute | solution.py:209
  60.6 21.7 %all-to-all-start.3 = ((f32[32,40,128]{2,1,0:T(8,128)}), f32[32,40,128]{2,1,0:T(8,128)S(1)}, u32[]{:S(2)}, u32[]{:S(2)}) async-start(f32[32,40,128]{2,1,0:T(8,128)} %broadcast_in_dim.10), calls=%async_computation.3 | async-start | bytes 1310720 | tf_op jit(solution)/shard_map/all_to_all | solution.py:205
  64.5 1.6 %copy-start.1 = (f32[1024,512]{1,0:T(8,128)S(1)}, f32[1024,512]{1,0:T(8,128)}, u32[]{:S(2)}) copy-start(f32[1024,512]{1,0:T(8,128)} %all-gather.2.cloned.1.call-done.p_ref) | copy-start | bytes 6291460
  66.8 6.6 %collective-permute-start.1 = (f32[128,256]{1,0:T(8,128)S(1)}, f32[128,256]{1,0:T(8,128)S(1)}, u32[]{:S(2)}, u32[]{:S(2)}) collective-permute-start(f32[128,256]{1,0:T(8,128)S(1)} %get-tuple-element.15), channel_id=1, source_target_pairs={{0,256},{256,0},{1,257},{257,1},{2,258},{258,2},{3,259},{259,3},{4... | collective-permute-start | bytes 393224 | tf_op jit(solution)/shard_map/ppermute | solution.py:209
  73.5 6.6 %collective-permute-start.2 = (f32[128,256]{1,0:T(8,128)S(1)}, f32[128,256]{1,0:T(8,128)S(1)}, u32[]{:S(2)}, u32[]{:S(2)}) collective-permute-start(f32[128,256]{1,0:T(8,128)S(1)} %add.10), channel_id=1, source_target_pairs={{0,32},{32,0},{64,96},{96,64},{128,160},{160,128},{192,224},{224,1... | collective-permute-start | bytes 393224 | tf_op jit(solution)/shard_map/ppermute | solution.py:307
  82.3 1.0 copy-start.3
  83.3 22.9 %all-to-all-start.4 = ((f32[4,128,256]{2,1,0:T(8,128)}), f32[4,128,256]{2,1,0:T(8,128)}, u32[]{:S(2)}, u32[]{:S(2)}) async-start(f32[4,128,256]{2,1,0:T(8,128)} %broadcast_in_dim.11), calls=%async_computation.4 | async-start | bytes 1048576 | tf_op jit(solution)/shard_map/all_to_all | solution.py:205
  91.2 1.1 copy-start.4
  92.3 19.2 %copy-start.2 = (f32[1024,512]{1,0:T(8,128)S(1)}, f32[1024,512]{1,0:T(8,128)}, u32[]{:S(2)}) copy-start(f32[1024,512]{1,0:T(8,128)} %all-gather.2.cloned.1.call-done.p_ref) | copy-start | bytes 6291460
  107.3 4.2 %collective-permute-start.3 = (f32[128,256]{1,0:T(8,128)S(1)}, f32[128,256]{1,0:T(8,128)S(1)}, u32[]{:S(2)}, u32[]{:S(2)}) collective-permute-start(f32[128,256]{1,0:T(8,128)S(1)} %reduce_sum.29.kept_ref), channel_id=1, source_target_pairs={{0,256},{256,0},{1,257},{257,1},{2,258},{258,2},{3,259},{259,3},{4... | collective-permute-start | bytes 393224 | tf_op jit(solution)/shard_map/ppermute | solution.py:209
  111.5 1.0 copy-start.6
Sparse Core Ops, SparseCore 0:
  18.6 44.8 all-gather.1
